TPU v7x, 128 devices: a whole 4x4x4 slice. The times are simulated.
128 devices in a mesh: tok: 32 (over z, y, core), pb: 4 (over x).
Axes of the slice: x: 4, y: 4, z: 4, core: 2. Of those that a mesh axis runs over, the one named last changes fastest.
Arguments:
- activations: bfloat16 [65536, 14336], P('tok', 'pb'), may hold values from -6 to 6
- out_grads: bfloat16 [65536, 4096], P('tok', 'pb'), may hold values from -6 to 6
- proj_in: bfloat16 [14336, 64], P('pb'), may hold values from -0.046875 to 0.046875
- proj_out: bfloat16 [4096, 64], P('pb'), may hold values from -0.09375 to 0.09375
- doc_starts: int32 [512], replicated, may hold values from 0 to 65535, as said below
- doc_owner: int32 [512], replicated, may hold values from 0 to 31, as said below
- queries: bfloat16 [8192, 4096], P('pb', 'tok'), may hold values from -6 to 6
Outputs:
- scores: float32 [512, 8192], P('tok', 'pb')
Inputs may be any that keep to these rules, and one draw needn't show every extreme that they name: doc_starts[0] is 0 and the offsets rise strictly; document d holds tokens doc_starts[d] to doc_starts[d+1] - 1, the last one up to 65535, and the last document is the single token 65535; no document but the first starts at a multiple of 512; the tokens of one aligned block of 512 belong to at most 9 documents, and in some block to exactly 9. `doc_owner`: the documents form runs of 32 consecutive ones starting at multiples of 32, each run naming every owner index once, and the last document of a run has the owner of the first document of the next run; among the documents with tokens in one aligned block of 512 tokens at most 2 have one owner, and in some block exactly 2.
All inputs are finite; a program needn't handle non-finite values.
Results may differ from a plain program's by a relative error of at most 0.013.
Values may be sent and summed in bfloat16 or wider, within the bound.
A program may use at most 128 MiB of HBM per device.

v0:
```python
import jax
import jax.numpy as jnp
from jax import lax
from jax.sharding import PartitionSpec as P

WIN = 9


EPS = 1e-06


def doc_ranks(doc_owner, per_owner):
    doc_count = doc_owner.shape[0]
    doc_order = jnp.arange(doc_count, dtype=jnp.int32)
    same_owner = (doc_owner[None, :] == doc_owner[:, None]) & (
        doc_order[None, :] < doc_order[:, None]
    )
    return doc_owner * per_owner + jnp.sum(same_owner.astype(jnp.int32), axis=1)


def window_slots(block_ids, block_rows, doc_starts, rank_all):
    doc_count = doc_starts.shape[0]
    firsts = block_ids * block_rows
    lasts = firsts + block_rows - 1
    first_doc = jnp.sum((doc_starts[None, :] <= firsts[:, None]).astype(jnp.int32), axis=1) - 1
    last_doc = jnp.sum((doc_starts[None, :] <= lasts[:, None]).astype(jnp.int32), axis=1) - 1
    slot_docs = first_doc[:, None] + jnp.arange(WIN, dtype=jnp.int32)[None, :]
    doc_ids = jnp.arange(doc_count, dtype=jnp.int32)
    matches = slot_docs[:, :, None] == doc_ids[None, None, :]
    slot_rank = jnp.sum(jnp.where(matches, rank_all[None, None, :], 0), axis=2)
    return (first_doc, jnp.where(slot_docs <= last_doc[:, None], slot_rank, doc_count))


def per_device(activations, out_grads, proj_in, proj_out, doc_starts, doc_owner, queries):
    group_count = lax.axis_size("pb")
    owner_count = lax.axis_size("tok")
    tok_rows = activations.shape[0]
    block_rows = tok_rows // group_count
    proj_width = proj_in.shape[1]
    doc_count = doc_starts.shape[0]
    per_owner = doc_count // owner_count
    projected = lax.psum_scatter(
        jnp.concatenate(
            [
                jnp.dot(activations, proj_in, preferred_element_type=jnp.float32),
                jnp.dot(out_grads, proj_out, preferred_element_type=jnp.float32),
            ],
            axis=1,
        ),
        "pb",
        scatter_dimension=0,
        tiled=True,
    ).astype(jnp.bfloat16)
    act_proj = projected[:, :proj_width]
    grad_proj = projected[:, proj_width:]
    block_index = lax.axis_index("tok") * group_count + lax.axis_index("pb")
    rank_all = doc_ranks(doc_owner, per_owner)
    first_doc, slot_rank = window_slots(block_index[None], block_rows, doc_starts, rank_all)
    positions = block_index * block_rows + jnp.arange(block_rows, dtype=jnp.int32)
    doc_index = jnp.sum((doc_starts[None, :] <= positions[:, None]).astype(jnp.int32), axis=1) - 1
    local_slot = doc_index - first_doc[0]
    onehot = (local_slot[:, None] == jnp.arange(WIN, dtype=jnp.int32)[None, :]).astype(jnp.bfloat16)
    weighted = (onehot[:, :, None] * grad_proj[:, None, :]).reshape(block_rows, WIN * proj_width)
    window_grads = jnp.einsum(
        "tk,ts->ks", weighted, act_proj, preferred_element_type=jnp.float32
    ).reshape(WIN, proj_width * proj_width)
    doc_ids = jnp.arange(doc_count, dtype=jnp.int32)
    placement = (doc_ids[:, None] == slot_rank[0][None, :]).astype(jnp.float32)
    ordered = jnp.dot(placement, window_grads, precision=lax.Precision.HIGHEST)
    owner_sums = lax.psum_scatter(ordered, "tok", scatter_dimension=0, tiled=True)
    summed = lax.psum(owner_sums, "pb")
    norm_sizes = jnp.sqrt(jnp.sum(summed * summed, axis=1, keepdims=True) + EPS)
    unit_rows = (summed / norm_sizes).astype(jnp.bfloat16)
    return jnp.dot(
        unit_rows,
        lax.all_gather(queries, "tok", axis=1, tiled=True).T,
        preferred_element_type=jnp.float32,
    )


def solution(mesh):
    in_specs = (
        P("tok", "pb"),
        P("tok", "pb"),
        P("pb", None),
        P("pb", None),
        P(),
        P(),
        P("pb", "tok"),
    )
    out_specs = P("tok", "pb")
    return jax.shard_map(
        per_device, mesh=mesh, in_specs=in_specs, out_specs=out_specs, check_vma=False
    )
```

profile of v0, /device:TPU:1, one launch (start us, length us, event | category | flops | bytes accessed | tf_op | source)
XLA Modules:
  0.0 292.8 jit_solution(3617274717339050857)
XLA Ops:
  6.5 0.0 copy-start
  6.5 0.0 copy-start.2
  6.5 0.0 copy-start.1
  6.5 0.0 reduce-scatter.3.cloned.1.call-start
  6.5 3.6 %fusion.10 = f32[2048,64]{0,1:T(8,128)S(1)} fusion(bf16[2048,1024]{1,0:T(8,128)(2,1)} %param.8, bf16[1024,64]{0,1:T(8,128)(2,1)} %param.10), kind=kOutput, calls=%fused_computation.28 | convolution fusion | flops 268435456 | bytes 4849664 | tf_op jit(solution)/shard_map/dot_general | solution.py:46
  10.2 0.0 copy-done
  10.2 9.7 %fusion.9 = f32[2048,64]{0,1:T(8,128)S(1)} fusion(bf16[2048,3584]{1,0:T(8,128)(2,1)} %param.7, bf16[3584,64]{0,1:T(8,128)(2,1)S(1)} %copy-done), kind=kOutput, calls=%fused_computation.27 | convolution fusion | flops 939524096 | bytes 15663104 | tf_op jit(solution)/shard_map/dot_general | solution.py:45
  19.9 1.1 pad_maximum_fusion
  20.9 0.0 reduce-scatter.3.cloned.1.call-update
  21.0 0.0 reduce-scatter.5.cloned.1.call-start
  21.0 0.0 copy-done.2
  21.0 0.7 convert_reduce_fusion.2
  23.0 0.0 copy-done.1
  23.0 0.2 convert_reduce_fusion.1
  23.3 0.3 fusion.8
  23.6 0.3 convert_reduce_fusion
  23.9 22.6 %reduce-scatter.3.cloned.1.call-done = f32[512,128]{0,1:T(8,128)} async-done(((f32[2048,128]{0,1:T(8,128)}), f32[512,128]{0,1:T(8,128)}) %reduce-scatter.3.cloned.1.call-update) | async-done | bytes 262160 | tf_op jit(solution)/shard_map/reduce_scatter | solution.py:42
  46.5 1.0 convert_element_type.33
  47.5 0.3 fusion.5
  47.8 0.1 reshape.153
  48.0 5.6 %fusion.1 = f32[512,4096]{1,0:T(8,128)} fusion(f32[9,4096]{1,0:T(8,128)S(1)} %reshape.153, s32[9]{0:T(128)S(1)} %compare_select_fusion.1), kind=kOutput, calls=%fused_computation.9 | convolution fusion | flops 226497024 | bytes 8536100 | tf_op jit(solution)/shard_map/dot_general | solution.py:69
  53.6 0.0 reduce-scatter.5.cloned.1.call-update
  53.6 0.0 all-reduce.2.cloned.1.call-start
  53.7 92.4 %reduce-scatter.5.cloned.1.call-done = f32[16,4096]{1,0:T(8,128)} async-done(((f32[512,4096]{1,0:T(8,128)}), f32[16,4096]{1,0:T(8,128)}) %reduce-scatter.5.cloned.1.call-update) | async-done | bytes 262160 | tf_op jit(solution)/shard_map/reduce_scatter | solution.py:70
  146.0 0.0 all-reduce.2.cloned.1.call-update
  146.0 0.0 all-gather.2.cloned.1.call-start
  146.1 0.5 all-gather.2.cloned.1.call-update
  146.6 42.1 %all-reduce.2.cloned.1.call-done = f32[16,4096]{1,0:T(8,128)} async-done(((f32[16,4096]{1,0:T(8,128)}), f32[16,4096]{1,0:T(8,128)}) %all-reduce.2.cloned.1.call-update) | async-done | bytes 262160 | tf_op jit(solution)/shard_map/psum | solution.py:71
  188.8 1.1 multiply_reduce_fusion
  189.9 85.5 %all-gather.2.cloned.1.call-done = bf16[2048,4096]{1,0:T(8,128)(2,1)} async-done(((bf16[2048,128]{1,0:T(8,128)(2,1)}), bf16[2048,4096]{1,0:T(8,128)(2,1)}) %all-gather.2.cloned.1.call-update) | async-done | bytes 16777232 | tf_op jit(solution)/shard_map/all_gather | solution.py:76
  275.3 11.0 %fusion.2 = f32[16,2048]{1,0:T(8,128)} fusion(bf16[2048,4096]{1,0:T(8,128)(2,1)} %all-gather.2.cloned.1.call-done, f32[16,4096]{1,0:T(8,128)} %all-reduce.2.cloned.1.call-done, f32[16]{0:T(128)S(1)} %add_sqrt_fusion), kind=kOutput, calls=%fused_computation.10 | convolution fusion | flops 268566528 | bytes 17170496 | tf_op jit(solution)/shard_map/dot_general | solution.py:74
  (8 shorter events, 0.1 us)
Async XLA Ops:
  6.5 3.6 %copy-start = (bf16[3584,64]{0,1:T(8,128)(2,1)S(1)}, bf16[3584,64]{0,1:T(8,128)(2,1)}, u32[]{:S(2)}) copy-start(bf16[3584,64]{0,1:T(8,128)(2,1)} %param.9) | copy-start | bytes 1376260
  6.5 14.5 %copy-start.2 = (s32[512]{0:T(512)S(1)}, s32[512]{0:T(512)}, u32[]{:S(2)}) copy-start(s32[512]{0:T(512)} %param.11) | copy-start | bytes 6148
  6.5 16.5 %copy-start.1 = (s32[512]{0:T(512)S(1)}, s32[512]{0:T(512)}, u32[]{:S(2)}) copy-start(s32[512]{0:T(512)} %param.12) | copy-start | bytes 6148
  6.5 40.0 %reduce-scatter.3.cloned.1.call-start = ((), (), s32[]{:S(2)}) async-start(), calls=%async_computation.2 | async-start | bytes 1310720 | tf_op jit(solution)/shard_map/reduce_scatter | solution.py:42
  21.0 125.1 %reduce-scatter.5.cloned.1.call-start = ((), (), s32[]{:S(2)}) async-start(), calls=%async_computation.3 | async-start | bytes 8650752 | tf_op jit(solution)/shard_map/reduce_scatter | solution.py:70
  53.6 135.2 %all-reduce.2.cloned.1.call-start = ((), (), s32[]{:S(2)}) async-start(), calls=%async_computation.4 | async-start | bytes 524288 | tf_op jit(solution)/shard_map/psum | solution.py:71
  146.0 129.3 %all-gather.2.cloned.1.call-start = ((), (), s32[]{:S(2)}) async-start(), calls=%async_computation.5 | async-start | bytes 17301504 | tf_op jit(solution)/shard_map/all_gather | solution.py:76
Sparse Core Ops, SparseCore 0:
  21.1 25.3 reduce-scatter.2
  53.7 92.2 reduce-scatter.4
  148.4 40.3 all-reduce.1
  191.0 84.2 all-gather.1
where the time goes:
time: 293 us
  waiting for transfers between devices  243 us (83%)
  matrix products  30.2 us (10%)
  between operations  14.5 us (5%)
  other arithmetic  4.73 us (2%)
    reduce_scatter x1, waiting for transfers between devices, per_device(): lax.psum_scatter(ordered, 'tok', scatter_dimension=0, tiled=True)  92.4 us
    all_gather x1, waiting for transfers between devices, per_device(): lax.all_gather(queries, 'tok', axis=1, tiled=True)  85.5 us
    psum x1, waiting for transfers between devices, per_device(): summed = lax.psum(owner_sums, 'pb')  42.1 us
    reduce_scatter x1, waiting for transfers between devices, per_device(): lax.psum_scatter(jnp.concatenate([jnp.dot(activations, proj_in, preferred...  22.6 us
    dot_general x1, matrix products, per_device(): jnp.dot(unit_rows, lax.all_gather(queries, 'tok', axis=1, tiled=True).T,...  11 us
    dot_general x1, matrix products, per_device(): jnp.dot(activations, proj_in, preferred_element_type=jnp.float32)  9.67 us
  transfers between devices with their start and end apart: 4, of which 4 were waited for; matrix products, arithmetic and copies ran while one was open for 1% of the time, Pallas kernels for 0%

commit v1 on v0

v1 whole, which is shorter than its diff:
```python
import functools

import jax
import jax.numpy as jnp
from jax import lax
from jax.experimental import pallas as pl
from jax.experimental.pallas import tpu as pltpu
from jax.sharding import PartitionSpec as P

EPS = 1e-06
SHARE = 512
SLOTS = 16
SUB = 256
MESH = pl.DeviceIdType.MESH
HOPS = (2, 1, 3, 0)
NT = (((1,), (1,)), ((), ()))
F32 = jnp.float32
BF16 = jnp.bfloat16


def remote(src, dst, send_sem, recv_sem, tok, pb):
    return pltpu.make_async_remote_copy(
        src_ref=src,
        dst_ref=dst,
        send_sem=send_sem,
        recv_sem=recv_sem,
        device_id=(tok, pb),
        device_id_type=MESH,
    )


def kernel(
    act_hbm,
    grad_hbm,
    win_hbm,
    wout_hbm,
    starts_ref,
    owner_ref,
    q_hbm,
    out_ref,
    act_buf,
    grad_buf,
    win,
    wout,
    proj_send,
    proj_own,
    proj_recv,
    proj_t,
    onehot_ref,
    place,
    lhs,
    wnd,
    wnd_recv,
    part_send,
    part_recv,
    units,
    va,
    vb,
    qa,
    qb,
    fa,
    fb,
    fa_recv,
    fb_recv,
    load_sem,
    w_sem,
    q_sem,
    qs_send,
    qs_recv,
    p_send,
    p_recv,
    w_send,
    w_recv,
    x_send,
    x_recv,
    u_send,
    u_recv,
    f_send,
    f_recv,
):
    tok = lax.axis_index("tok")
    pb = lax.axis_index("pb")
    z, y, c = tok // 8, (tok // 2) % 4, tok % 2
    steps = act_buf.shape[0]
    per_hop = steps // 4

    loads = [
        pltpu.make_async_copy(win_hbm, win, w_sem.at[0]),
        pltpu.make_async_copy(wout_hbm, wout, w_sem.at[1]),
    ]
    for copy in loads:
        copy.start()
    for s in range(steps):
        row = ((pb + HOPS[s // per_hop]) % 4) * SHARE + (s % per_hop) * SUB
        rows = pl.ds(pl.multiple_of(row, SUB), SUB)
        pltpu.make_async_copy(act_hbm.at[rows], act_buf.at[s], load_sem.at[0, s]).start()
        pltpu.make_async_copy(grad_hbm.at[rows], grad_buf.at[s], load_sem.at[1, s]).start()
        if s == 1:
            pltpu.make_async_copy(q_hbm.at[pl.ds(0, 1024)], qa.at[y], q_sem.at[0]).start()
            pltpu.make_async_copy(q_hbm.at[pl.ds(1024, 1024)], qb.at[z], q_sem.at[1]).start()

    barrier = pltpu.get_barrier_semaphore()
    for n in range(1, 4):
        pl.semaphore_signal(barrier, inc=1, device_id=(tok, (pb + n) % 4), device_id_type=MESH)

    @pl.loop(1, 32)
    def _(n):
        pl.semaphore_signal(barrier, inc=1, device_id=((tok + n) % 32, pb), device_id_type=MESH)

    token = (tok * 4 + pb) * SHARE
    starts = starts_ref[...]
    begun = starts <= token + lax.broadcasted_iota(jnp.int32, (SHARE, 512), 0)
    doc_lane = lax.broadcasted_iota(jnp.int32, (SLOTS, 512), 1)
    slot_row = lax.broadcasted_iota(jnp.int32, (SLOTS, 512), 0)
    enters = (doc_lane % SLOTS == slot_row).astype(F32)
    leaves = ((doc_lane > 0) & ((doc_lane + SLOTS - 1) % SLOTS == slot_row)).astype(F32)
    onehot_ref[...] = lax.dot_general(
        (enters - leaves).astype(BF16), begun.astype(F32).astype(BF16), NT, preferred_element_type=F32
    )
    lane8 = lax.broadcasted_iota(jnp.int32, (8, 512), 1)
    row8 = lax.broadcasted_iota(jnp.int32, (8, 512), 0)
    first = jnp.broadcast_to(starts, (8, 512)) // SHARE
    last = jnp.where(lane8 == 511, 127, pltpu.roll(first, 511, 1))
    facts = jnp.where(row8 == 0, first, jnp.where(row8 == 1, last, lane8 % SLOTS))
    rank = owner_ref[...] * 16 + lax.broadcasted_iota(jnp.int32, (1, 512), 1) // 32
    perm = (rank == lax.broadcasted_iota(jnp.int32, (512, 512), 0)).astype(F32).astype(BF16)
    ranked = lax.dot_general(perm, facts.astype(F32).astype(BF16), NT, preferred_element_type=F32)
    col = lax.broadcasted_iota(jnp.int32, (512, 512), 1)
    block = ((col // SLOTS) * 4 + pb).astype(F32)
    slot = (col % SLOTS).astype(F32)
    inside = (ranked[:, 0:1] <= block) & (block <= ranked[:, 1:2]) & (ranked[:, 2:3] == slot)
    place[...] = inside.astype(F32).astype(BF16)

    pl.semaphore_wait(barrier, 34)

    for h in range(2):
        pltpu.make_async_copy(q_hbm.at[pl.ds(0, 1024)], qa.at[0], q_sem.at[h]).wait()
    q_copies = []
    for n in range(1, 4):
        to_y = z * 8 + ((y + n) % 4) * 2 + c
        to_z = ((z + n) % 4) * 8 + y * 2 + c
        q_copies.append(remote(qa.at[y], qa.at[y], qs_send.at[0, n - 1], qs_recv.at[0, n - 1], to_y, pb))
        q_copies.append(remote(qb.at[z], qb.at[z], qs_send.at[1, n - 1], qs_recv.at[1, n - 1], to_z, pb))
    for copy in q_copies:
        copy.start()

    for copy in loads:
        copy.wait()

    @pl.loop(0, steps)
    def _(s):
        pltpu.make_async_copy(act_hbm.at[pl.ds(0, SUB)], act_buf.at[s], load_sem.at[0, s]).wait()
        pltpu.make_async_copy(grad_hbm.at[pl.ds(0, SUB)], grad_buf.at[s], load_sem.at[1, s]).wait()
        both = jnp.concatenate(
            [
                jnp.dot(act_buf[s], win[...], preferred_element_type=F32),
                jnp.dot(grad_buf[s], wout[...], preferred_element_type=F32),
            ],
            axis=1,
        )

        @pl.when(s < 3 * per_hop)
        def _():
            proj_send[s] = both.astype(BF16)
            q = s // per_hop
            hop = jnp.where(q == 0, HOPS[0], jnp.where(q == 1, HOPS[1], HOPS[2]))
            remote(
                proj_send.at[s], proj_recv.at[s], p_send.at[s], p_recv.at[s], tok, (pb + hop) % 4
            ).start()

        @pl.when(s >= 3 * per_hop)
        def _():
            proj_own[s - 3 * per_hop] = both

    proj_copies = [
        remote(proj_send.at[s], proj_recv.at[s], p_send.at[s], p_recv.at[s], tok, (pb + HOPS[s // per_hop]) % 4)
        for s in range(3 * per_hop)
    ]
    for copy in proj_copies:
        copy.wait_recv()
    sums = []
    for h in range(per_hop):
        total = proj_own[h]
        for q in range(3):
            total = total + proj_recv[q * per_hop + h].astype(F32)
        sums.append(total)
    proj = jnp.concatenate(sums, axis=0).astype(BF16).astype(F32)

    proj_t[...] = proj.T[64:128, :]
    onehot = onehot_ref[...]
    for r in range(64):
        picked = onehot * proj_t[r : r + 1, :]
        lhs[pl.ds((r // 2) * SLOTS, SLOTS), pl.ds((r % 2) * SHARE, SHARE)] = picked.astype(BF16)
    low = lax.broadcasted_iota(jnp.int32, (SHARE, 128), 1) < 64
    rhs = jnp.concatenate(
        [jnp.where(low, proj, 0.0), jnp.where(low, 0.0, pltpu.roll(proj, 64, 1))], axis=0
    ).astype(BF16)
    wnd[...] = jnp.dot(lhs[...], rhs, preferred_element_type=F32).astype(BF16)

    @pl.loop(1, 32)
    def _(n):
        to = (tok + n) % 32
        remote(
            wnd.at[pl.ds(pl.multiple_of(to * SLOTS, SLOTS), SLOTS)],
            wnd_recv.at[pl.ds(pl.multiple_of(tok * SLOTS, SLOTS), SLOTS)],
            w_send,
            w_recv,
            to,
            pb,
        ).start()

    mine = pl.ds(pl.multiple_of(tok * SLOTS, SLOTS), SLOTS)
    wnd_recv[mine, :] = wnd[mine, :]
    others = pl.ds(0, 31 * SLOTS)
    pltpu.make_async_copy(wnd_recv.at[others], wnd_recv.at[others], w_recv).wait()
    part = jnp.dot(place[...], wnd_recv[...], preferred_element_type=F32)
    part_send[...] = part.astype(BF16)
    x_copies = [
        remote(part_send, part_recv.at[n - 1], x_send.at[n - 1], x_recv.at[n - 1], tok, (pb + n) % 4)
        for n in range(1, 4)
    ]
    for copy in x_copies:
        copy.start()
    for copy in x_copies:
        copy.wait_recv()
    for n in range(3):
        part = part + part_recv[n].astype(F32)
    units[...] = part.astype(BF16).reshape(4, 4, 32, 128)

    u_copies = []
    for n in range(1, 4):
        ty, tz = (y + n) % 4, (z + n) % 4
        u_copies.append(
            remote(units.at[:, ty], va.at[y], u_send.at[0, n - 1], u_recv.at[0, n - 1], z * 8 + ty * 2 + c, pb)
        )
        u_copies.append(
            remote(units.at[tz], vb.at[z], u_send.at[1, n - 1], u_recv.at[1, n - 1], tz * 8 + y * 2 + c, pb)
        )
    for copy in u_copies:
        copy.start()
    va[y] = units[:, y]
    vb[z] = units[z]
    for copy in q_copies:
        copy.wait_recv()

    def scores(v, q):
        total = jnp.zeros((128, 1024), F32)
        for n in range(4):
            total = total + lax.dot_general(v[n].reshape(128, 128), q[n], NT, preferred_element_type=F32)
        return total.astype(BF16)

    for copy in u_copies[0::2]:
        copy.wait_recv()
    fa[:, :1024] = scores(va, qa)
    squares = jnp.zeros((128, 128), F32)
    for n in range(4):
        v = va[n].reshape(128, 128).astype(F32)
        squares = squares + v * v
    square = jnp.broadcast_to(jnp.sum(squares, axis=1, keepdims=True), (128, 128))
    high = square.astype(BF16)
    rest = (square - high.astype(F32)).astype(BF16)
    fa[:, 1024:] = jnp.where(lax.broadcasted_iota(jnp.int32, (128, 128), 1) < 64, high.astype(F32), rest.astype(F32)).astype(
        BF16
    )
    fa_me, fb_me = z * 2 + c, y * 2 + c

    @pl.loop(1, 8)
    def _(n):
        to = (fa_me + n) % 8
        remote(
            fa.at[pl.ds(pl.multiple_of(to * 16, 16), 16)],
            fa_recv.at[fa_me],
            f_send.at[0],
            f_recv.at[0],
            (to // 2) * 8 + y * 2 + to % 2,
            pb,
        ).start()

    for copy in u_copies[1::2]:
        copy.wait_recv()
    fb[...] = scores(vb, qb)

    @pl.loop(1, 8)
    def _(n):
        to = (fb_me + n) % 8
        remote(
            fb.at[pl.ds(pl.multiple_of(to * 16, 16), 16)],
            fb_recv.at[fb_me],
            f_send.at[1],
            f_recv.at[1],
            z * 8 + to,
            pb,
        ).start()

    fa_recv[fa_me] = fa[pl.ds(pl.multiple_of(fa_me * 16, 16), 16), :]
    fb_recv[fb_me] = fb[pl.ds(pl.multiple_of(fb_me * 16, 16), 16), :]
    pltpu.make_async_copy(fa_recv.at[pl.ds(0, 7)], fa_recv.at[pl.ds(0, 7)], f_recv.at[0]).wait()
    total_a = jnp.zeros((16, 1152), F32)
    for n in range(8):
        total_a = total_a + fa_recv[n].astype(F32)
    tail = total_a[:, 1024:]
    norm = lax.rsqrt(tail + pltpu.roll(tail, 64, 1) + EPS)[:, 0:1]
    out_ref[:, :1024] = total_a[:, :1024] * norm
    pltpu.make_async_copy(fb_recv.at[pl.ds(0, 7)], fb_recv.at[pl.ds(0, 7)], f_recv.at[1]).wait()
    total_b = jnp.zeros((16, 1024), F32)
    for n in range(8):
        total_b = total_b + fb_recv[n].astype(F32)
    out_ref[:, 1024:] = total_b * norm

    for copy in q_copies + proj_copies + x_copies + u_copies:
        copy.wait_send()
    pltpu.make_async_copy(wnd.at[others], wnd.at[others], w_send).wait()
    pltpu.make_async_copy(fa.at[pl.ds(0, 112)], fa.at[pl.ds(0, 112)], f_send.at[0]).wait()
    pltpu.make_async_copy(fb.at[pl.ds(0, 112)], fb.at[pl.ds(0, 112)], f_send.at[1]).wait()


def per_device(activations, out_grads, proj_in, proj_out, doc_starts, doc_owner, queries):
    any_spec = pl.BlockSpec(memory_space=pl.ANY)
    vmem_spec = pl.BlockSpec(memory_space=pltpu.VMEM)
    depth_in, depth_out = activations.shape[1], out_grads.shape[1]
    steps = activations.shape[0] // SUB
    per_hop = steps // 4
    dma = pltpu.SemaphoreType.DMA
    return pl.pallas_call(
        kernel,
        out_shape=jax.ShapeDtypeStruct((16, 2048), F32),
        in_specs=[any_spec, any_spec, any_spec, any_spec, vmem_spec, vmem_spec, any_spec],
        out_specs=vmem_spec,
        scratch_shapes=[
            pltpu.VMEM((steps, SUB, depth_in), BF16),
            pltpu.VMEM((steps, SUB, depth_out), BF16),
            pltpu.VMEM((depth_in, 64), BF16),
            pltpu.VMEM((depth_out, 64), BF16),
            pltpu.VMEM((3 * per_hop, SUB, 128), BF16),
            pltpu.VMEM((per_hop, SUB, 128), F32),
            pltpu.VMEM((3 * per_hop, SUB, 128), BF16),
            pltpu.VMEM((64, SHARE), F32),
            pltpu.VMEM((SLOTS, SHARE), F32),
            pltpu.VMEM((512, 512), BF16),
            pltpu.VMEM((512, 2 * SHARE), BF16),
            pltpu.VMEM((512, 128), BF16),
            pltpu.VMEM((512, 128), BF16),
            pltpu.VMEM((512, 128), BF16),
            pltpu.VMEM((3, 512, 128), BF16),
            pltpu.VMEM((4, 4, 32, 128), BF16),
            pltpu.VMEM((4, 4, 32, 128), BF16),
            pltpu.VMEM((4, 4, 32, 128), BF16),
            pltpu.VMEM((4, 1024, 128), BF16),
            pltpu.VMEM((4, 1024, 128), BF16),
            pltpu.VMEM((128, 1152), BF16),
            pltpu.VMEM((128, 1024), BF16),
            pltpu.VMEM((8, 16, 1152), BF16),
            pltpu.VMEM((8, 16, 1024), BF16),
            dma((2, steps)),
            dma((2,)),
            dma((2,)),
            dma((2, 3)),
            dma((2, 3)),
            dma((3 * per_hop,)),
            dma((3 * per_hop,)),
            dma,
            dma,
            dma((3,)),
            dma((3,)),
            dma((2, 3)),
            dma((2, 3)),
            dma((2,)),
            dma((2,)),
        ],
        compiler_params=pltpu.CompilerParams(
            collective_id=0, has_side_effects=True, vmem_limit_bytes=52 * 1024 * 1024
        ),
    )(
        activations,
        out_grads,
        proj_in,
        proj_out,
        doc_starts.reshape(1, 512),
        doc_owner.reshape(1, 512),
        queries,
    )


def solution(mesh):
    in_specs = (
        P("tok", "pb"),
        P("tok", "pb"),
        P("pb", None),
        P("pb", None),
        P(),
        P(),
        P("pb", "tok"),
    )
    return jax.shard_map(
        per_device, mesh=mesh, in_specs=in_specs, out_specs=P("tok", "pb"), check_vma=False
    )
```

time: 293 us -> 50.9 us (0.17)
  waiting for transfers between devices: 243 us -> 0 us
  Pallas kernels: 0 us -> 45 us
  matrix products: 30.2 us -> 0 us
  between operations: 14.5 us -> 0.03 us
  local copies, waits for them, and re-layouts: 0.14 us -> 5.58 us
  other arithmetic: 4.73 us -> 0 us
    reduce_scatter x2 -> x0, waiting for transfers between devices: 115 us -> none  [the longest x1 92.4 us: per_device(): lax.psum_scatter(ordered, 'tok', scatter_dimension=0, tiled=True)]
    all_gather x1 -> x0, waiting for transfers between devices: 85.5 us -> none  [per_device(): lax.all_gather(queries, 'tok', axis=1, tiled=True)]
    pallas_call x0 -> x1, Pallas kernels: none -> 45 us  [per_device(): pl.pallas_call(kernel, out_shape=jax.ShapeDtypeStruct((16, 2048), F32), i...]
    psum x1 -> x0, waiting for transfers between devices: 42.1 us -> none  [per_device(): summed = lax.psum(owner_sums, 'pb')]
    dot_general x5 -> x0, matrix products: 30.2 us -> none  [the longest x1 11 us: per_device(): jnp.dot(unit_rows, lax.all_gather(queries, 'tok', axis=1, tiled=True).T,...]
    unnamed x6 -> x9, local copies, waits for them, and re-layouts: 0.01 us -> 5.58 us
  transfers between devices with their start and end apart: 4 -> 0, of which waited for: 4 -> 0; matrix products, arithmetic and copies ran while one was open for 1% -> 0% of each run, Pallas kernels for 0% -> 0%
where the time goes in v1:
time: 50.9 us; the launch traced here: 50.6 us
  Pallas kernels  45 us (88%)
  local copies, waits for them, and re-layouts  5.58 us (11%)
    pallas_call x1, Pallas kernels, per_device(): pl.pallas_call(kernel, out_shape=jax.ShapeDtypeStruct((16, 2048), F32), i...  45 us
    unnamed x9, local copies, waits for them, and re-layouts  5.58 us

profile of v1, /device:TPU:1, one launch (start us, length us, event | category | flops | bytes accessed | tf_op | source)
XLA Modules:
  0.0 50.6 jit_solution(3999126150997480897)
XLA Ops:
  0.0 1.1 %copy.9.wout_hbm = bf16[1024,64]{1,0:T(8,128)(2,1)S(1)} copy(bf16[1024,64]{0,1:T(8,128)(2,1)} %param.10) | data formatting | bytes 262144 | tf_op args[3]
  1.1 1.4 %copy.8.win_hbm = bf16[3584,64]{1,0:T(8,128)(2,1)S(1)} copy(bf16[3584,64]{0,1:T(8,128)(2,1)} %param.9) | data formatting | bytes 917504 | tf_op args[2]
  2.5 0.0 copy-start
  2.5 1.0 %copy-done = bf16[2048,128]{1,0:T(8,128)(2,1)S(1)} copy-done((bf16[2048,128]{1,0:T(8,128)(2,1)S(1)}, bf16[2048,128]{1,0:T(8,128)(2,1)}, u32[]{:S(2)}) %copy-start) | copy-done | bytes 524312
  3.6 0.0 copy-start.1
  3.6 0.7 %copy-done.1 = s32[512]{0:T(512)S(1)} copy-done((s32[512]{0:T(512)S(1)}, s32[512]{0:T(512)}, u32[]{:S(2)}) %copy-start.1) | copy-done | bytes 2072
  4.3 0.0 copy-start.2
  4.3 0.7 %copy-done.2 = s32[512]{0:T(512)S(1)} copy-done((s32[512]{0:T(512)S(1)}, s32[512]{0:T(512)}, u32[]{:S(2)}) %copy-start.2) | copy-done | bytes 2072
  4.9 45.0 %shard_map.73 = f32[16,2048]{1,0:T(8,128)S(1)} custom-call(bf16[2048,3584]{1,0:T(8,128)(2,1)} %act_hbm.1, bf16[2048,1024]{1,0:T(8,128)(2,1)} %grad_hbm.1, bf16[3584,64]{1,0:T(8,128)(2,1)S(1)} %copy.8.win_hbm, bf16[1024,64]{1,0:T(8,128)(2,1)S(1)} %copy.9.wout_hbm, s32[1,512]{1,0:T(1,128)S(1)} %bitcast.2, s32[1,512]{1,0:T(1,128)S(1)} %bitcast.3, ...), custom_call_target="tpu_custom_call" | custom-call | tf_op jit(solution)/shard_map/pallas_call | solution.py:324
  49.9 0.7 %copy.11 = f32[16,2048]{1,0:T(8,128)} copy(f32[16,2048]{1,0:T(8,128)S(1)} %shard_map.73) | data formatting | bytes 262144
Async XLA Ops:
  2.5 1.0 %copy-start = (bf16[2048,128]{1,0:T(8,128)(2,1)S(1)}, bf16[2048,128]{1,0:T(8,128)(2,1)}, u32[]{:S(2)}) copy-start(bf16[2048,128]{1,0:T(8,128)(2,1)} %q_hbm.1) | copy-start | bytes 1572868
  3.6 0.7 %copy-start.1 = (s32[512]{0:T(512)S(1)}, s32[512]{0:T(512)}, u32[]{:S(2)}) copy-start(s32[512]{0:T(512)} %param.11) | copy-start | bytes 6148
  4.3 0.7 %copy-start.2 = (s32[512]{0:T(512)S(1)}, s32[512]{0:T(512)}, u32[]{:S(2)}) copy-start(s32[512]{0:T(512)} %param.12) | copy-start | bytes 6148

commit v2 on v1

v2 whole, which is shorter than its diff:
```python
import functools

import jax
import jax.numpy as jnp
from jax import lax
from jax.experimental import pallas as pl
from jax.experimental.pallas import tpu as pltpu
from jax.sharding import PartitionSpec as P

EPS = 1e-06
SHARE = 512
SLOTS = 16
MESH = pl.DeviceIdType.MESH
DEVICES = 128
NT = (((1,), (1,)), ((), ()))
F32 = jnp.float32
BF16 = jnp.bfloat16


def remote(src, dst, send_sem, recv_sem, tok, pb):
    return pltpu.make_async_remote_copy(
        src_ref=src,
        dst_ref=dst,
        send_sem=send_sem,
        recv_sem=recv_sem,
        device_id=(tok, pb),
        device_id_type=MESH,
    )


def hop_of(t):
    return jnp.where(t == 0, 2, jnp.where(t == 1, 1, jnp.where(t == 2, 3, 0)))


def kernel(
    act_hbm,
    grad_hbm,
    win_hbm,
    wout_hbm,
    starts_hbm,
    owner_hbm,
    q_hbm,
    out_ref,
    act_buf,
    grad_buf,
    win,
    wout,
    starts_ref,
    owner_ref,
    proj_send,
    proj_own,
    proj_recv,
    proj_t,
    onehot_ref,
    place,
    lhs,
    wnd,
    wnd_recv,
    units,
    va,
    vb,
    qa,
    qb,
    qa_t,
    qb_t,
    fa,
    fb,
    fa_recv,
    fb_recv,
    load_sem,
    w_sem,
    q_sem,
    qs_send,
    qs_recv,
    p_send,
    p_recv,
    d_send,
    d_recv,
    u_send,
    u_recv,
    f_send,
    f_recv,
):
    tok = lax.axis_index("tok")
    pb = lax.axis_index("pb")
    z, y, c = tok // 8, (tok // 2) % 4, tok % 2
    me = tok * 4 + pb

    def tile_loads(t):
        rows = pl.ds(pl.multiple_of(((pb + hop_of(t)) % 4) * SHARE, SHARE), SHARE)
        return [
            pltpu.make_async_copy(grad_hbm.at[rows], grad_buf.at[t], load_sem.at[0, t]),
            pltpu.make_async_copy(act_hbm.at[rows], act_buf.at[t], load_sem.at[1, t]),
        ]

    small = [
        pltpu.make_async_copy(wout_hbm, wout, w_sem.at[0]),
        pltpu.make_async_copy(win_hbm, win, w_sem.at[1]),
        pltpu.make_async_copy(starts_hbm, starts_ref, w_sem.at[2]),
        pltpu.make_async_copy(owner_hbm, owner_ref, w_sem.at[3]),
    ]
    q_loads = [
        pltpu.make_async_copy(q_hbm.at[pl.ds(0, 1024)], qa.at[y], q_sem.at[0]),
        pltpu.make_async_copy(q_hbm.at[pl.ds(1024, 1024)], qb.at[z], q_sem.at[1]),
    ]
    small[0].start()
    small[1].start()
    for copy in q_loads + tile_loads(0) + tile_loads(1):
        copy.start()
    small[2].start()
    small[3].start()

    barrier = pltpu.get_barrier_semaphore()

    planes = [lax.rem(pb + n, 4) for n in range(4)]
    for plane in planes[1:]:
        pl.semaphore_signal(barrier, inc=1, device_id=(tok, plane), device_id_type=MESH)

    @pl.loop(1, 32)
    def _(n):
        to = lax.rem(tok + n, 32)
        for plane in planes:
            pl.semaphore_signal(barrier, inc=1, device_id=(to, plane), device_id_type=MESH)

    q_copies = []
    for n in range(1, 4):
        to_y = z * 8 + ((y + n) % 4) * 2 + c
        to_z = ((z + n) % 4) * 8 + y * 2 + c
        q_copies.append(remote(qa.at[y], qa.at[y], qs_send.at[0, n - 1], qs_recv.at[0, n - 1], to_y, pb))
        q_copies.append(remote(qb.at[z], qb.at[z], qs_send.at[1, n - 1], qs_recv.at[1, n - 1], to_z, pb))

    pl.semaphore_wait(barrier, DEVICES - 1)
    for copy in q_loads:
        copy.wait()
    for copy in q_copies:
        copy.start()

    for copy in small[:2]:
        copy.wait()

    def proj_copy(t):
        return remote(
            proj_send.at[t], proj_recv.at[t], p_send.at[t], p_recv.at[t], tok, (pb + hop_of(t)) % 4
        )

    @pl.loop(0, 4)
    def _(t):
        @pl.when(t < 2)
        def _():
            for copy in tile_loads(t + 2):
                copy.start()

        for copy in tile_loads(t):
            copy.wait()
        both = jnp.concatenate(
            [
                lax.dot_general(act_buf[t], win[...], NT, preferred_element_type=F32),
                lax.dot_general(grad_buf[t], wout[...], NT, preferred_element_type=F32),
            ],
            axis=1,
        )

        @pl.when(t < 3)
        def _():
            proj_send[t] = both.astype(BF16)
            proj_copy(t).start()

        @pl.when(t == 3)
        def _():
            proj_own[...] = both

    for copy in small[2:]:
        copy.wait()
    starts = starts_ref[...]
    begun = starts <= me * SHARE + lax.broadcasted_iota(jnp.int32, (SHARE, 512), 0)
    doc_lane = lax.broadcasted_iota(jnp.int32, (SLOTS, 512), 1)
    slot_row = lax.broadcasted_iota(jnp.int32, (SLOTS, 512), 0)
    enters = (doc_lane % SLOTS == slot_row).astype(F32)
    leaves = ((doc_lane > 0) & ((doc_lane + SLOTS - 1) % SLOTS == slot_row)).astype(F32)
    onehot_ref[...] = lax.dot_general(
        (enters - leaves).astype(BF16), begun.astype(F32).astype(BF16), NT, preferred_element_type=F32
    )

    for t in range(3):
        proj_copy(t).wait_recv()
    proj = proj_own[...]
    for t in range(3):
        proj = proj + proj_recv[t].astype(F32)
    proj = proj.astype(BF16).astype(F32)

    proj_t[...] = proj.T[64:128, :]
    onehot = onehot_ref[...]
    for r in range(64):
        picked = onehot * proj_t[r : r + 1, :]
        lhs[pl.ds((r // 2) * SLOTS, SLOTS), pl.ds((r % 2) * SHARE, SHARE)] = picked.astype(BF16)
    low = lax.broadcasted_iota(jnp.int32, (SHARE, 128), 1) < 64
    rhs = jnp.concatenate(
        [jnp.where(low, proj, 0.0), jnp.where(low, 0.0, pltpu.roll(proj, 64, 1))], axis=0
    ).astype(BF16)
    wnd[...] = jnp.dot(lhs[...], rhs, preferred_element_type=F32).astype(BF16)

    mine = pl.ds(pl.multiple_of((me % 32) * SLOTS, SLOTS), SLOTS)

    def send_block(to, plane):
        remote(
            wnd.at[pl.ds(pl.multiple_of(to * SLOTS, SLOTS), SLOTS)],
            wnd_recv.at[z, mine],
            d_send,
            d_recv.at[z],
            to,
            plane,
        ).start()

    for plane in planes[1:]:
        send_block(tok, plane)

    @pl.loop(1, 32)
    def _(n):
        to = lax.rem(tok + n, 32)
        for plane in planes:
            send_block(to, plane)

    wnd_recv[z, mine, :] = wnd[pl.ds(pl.multiple_of(tok * SLOTS, SLOTS), SLOTS), :]

    lane8 = lax.broadcasted_iota(jnp.int32, (8, 512), 1)
    row8 = lax.broadcasted_iota(jnp.int32, (8, 512), 0)
    first = jnp.broadcast_to(starts, (8, 512)) // SHARE
    last = jnp.where(lane8 == 511, DEVICES - 1, pltpu.roll(first, 511, 1))
    facts = jnp.where(row8 == 0, first, jnp.where(row8 == 1, last, lane8 % SLOTS))
    rank = owner_ref[...] * 16 + lax.broadcasted_iota(jnp.int32, (1, 512), 1) // 32
    perm = (rank == lax.broadcasted_iota(jnp.int32, (512, 512), 0)).astype(F32).astype(BF16)
    ranked = lax.dot_general(perm, facts.astype(F32).astype(BF16), NT, preferred_element_type=F32)
    col = lax.broadcasted_iota(jnp.int32, (512, 512), 1)
    block = (col // SLOTS).astype(F32)
    own_slot = ranked[:, 2:3] == (col % SLOTS).astype(F32)

    @pl.loop(0, 4)
    def _(g):
        from_block = ranked[:, 0:1] - (g * 32).astype(F32)
        to_block = ranked[:, 1:2] - (g * 32).astype(F32)
        inside = (from_block <= block) & (block <= to_block) & own_slot
        place[g] = inside.astype(F32).astype(BF16)

    for copy in q_copies:
        copy.wait_recv()
    for n in range(4):
        qa_t[pl.ds(n * 128, 128), :] = qa[n].T
        qb_t[pl.ds(n * 128, 128), :] = qb[n].T

    summed = jnp.zeros((512, 128), F32)
    for n in (3, 2, 1, 0):
        g = (z + n) % 4
        got = wnd_recv.at[g, pl.ds(0, 512 if n else 496)]
        pltpu.make_async_copy(got, got, d_recv.at[g]).wait()
        summed = summed + jnp.dot(place[g], wnd_recv[g], preferred_element_type=F32)
    units[...] = summed.astype(BF16).reshape(4, 4, 32, 128)

    at_y = pl.ds(pl.multiple_of(y * 128, 128), 128)
    at_z = pl.ds(pl.multiple_of(z * 128, 128), 128)
    u_copies = []
    for n in range(1, 4):
        ty, tz = (y + n) % 4, (z + n) % 4
        u_copies.append(
            remote(
                units.at[tz], vb.at[:, :, at_z], u_send.at[1, n - 1], u_recv.at[1, n - 1], tz * 8 + y * 2 + c, pb
            )
        )
        u_copies.append(
            remote(
                units.at[:, ty], va.at[:, :, at_y], u_send.at[0, n - 1], u_recv.at[0, n - 1], z * 8 + ty * 2 + c, pb
            )
        )
    for copy in u_copies:
        copy.start()
    va[:, :, at_y] = units[:, y]
    vb[:, :, at_z] = units[z]
    fa_me, fb_me = z * 2 + c, y * 2 + c

    for copy in u_copies[0::2]:
        copy.wait_recv()
    fb[...] = jnp.dot(vb[...].reshape(128, 512), qb_t[...], preferred_element_type=F32).astype(BF16)

    @pl.loop(1, 8)
    def _(n):
        to = (fb_me + n) % 8
        remote(
            fb.at[pl.ds(pl.multiple_of(to * 16, 16), 16)],
            fb_recv.at[fb_me],
            f_send.at[1],
            f_recv.at[1],
            z * 8 + to,
            pb,
        ).start()

    for copy in u_copies[1::2]:
        copy.wait_recv()
    docs = va[...].reshape(128, 512)
    fa[:, :1024] = jnp.dot(docs, qa_t[...], preferred_element_type=F32).astype(BF16)
    wide = docs.astype(F32)
    square = jnp.broadcast_to(jnp.sum(wide * wide, axis=1, keepdims=True), (128, 128))
    high = square.astype(BF16).astype(F32)
    fa[:, 1024:] = jnp.where(
        lax.broadcasted_iota(jnp.int32, (128, 128), 1) < 64, high, square - high
    ).astype(BF16)

    @pl.loop(1, 8)
    def _(n):
        to = (fa_me + n) % 8
        remote(
            fa.at[pl.ds(pl.multiple_of(to * 16, 16), 16)],
            fa_recv.at[fa_me],
            f_send.at[0],
            f_recv.at[0],
            (to // 2) * 8 + y * 2 + to % 2,
            pb,
        ).start()

    fa_recv[fa_me] = fa[pl.ds(pl.multiple_of(fa_me * 16, 16), 16), :]
    fb_recv[fb_me] = fb[pl.ds(pl.multiple_of(fb_me * 16, 16), 16), :]
    pltpu.make_async_copy(fb_recv.at[pl.ds(0, 7)], fb_recv.at[pl.ds(0, 7)], f_recv.at[1]).wait()
    total_b = fb_recv[0].astype(F32)
    for n in range(1, 8):
        total_b = total_b + fb_recv[n].astype(F32)
    pltpu.make_async_copy(fa_recv.at[pl.ds(0, 7)], fa_recv.at[pl.ds(0, 7)], f_recv.at[0]).wait()
    total_a = fa_recv[0].astype(F32)
    for n in range(1, 8):
        total_a = total_a + fa_recv[n].astype(F32)
    tail = total_a[:, 1024:]
    norm = lax.rsqrt(tail + pltpu.roll(tail, 64, 1) + EPS)[:, 0:1]
    out_ref[:, :1024] = total_a[:, :1024] * norm
    out_ref[:, 1024:] = total_b * norm

    for t in range(3):
        proj_copy(t).wait_send()
    for copy in q_copies + u_copies:
        copy.wait_send()
    for g in range(4):
        some = wnd.at[pl.ds(0, 512 if g else 496)]
        pltpu.make_async_copy(some, some, d_send).wait()
    pltpu.make_async_copy(fa.at[pl.ds(0, 112)], fa.at[pl.ds(0, 112)], f_send.at[0]).wait()
    pltpu.make_async_copy(fb.at[pl.ds(0, 112)], fb.at[pl.ds(0, 112)], f_send.at[1]).wait()


def per_device(activations, out_grads, proj_in, proj_out, doc_starts, doc_owner, queries):
    depth_in, depth_out = activations.shape[1], out_grads.shape[1]
    dma = pltpu.SemaphoreType.DMA
    vmem = pltpu.VMEM

    def on_hbm(array):
        return pltpu.with_memory_space_constraint(array, pltpu.HBM)

    return pl.pallas_call(
        kernel,
        out_shape=jax.ShapeDtypeStruct((16, 2048), F32),
        in_specs=[pl.BlockSpec(memory_space=pltpu.HBM)] * 7,
        out_specs=pl.BlockSpec(memory_space=pltpu.VMEM),
        scratch_shapes=[
            vmem((4, SHARE, depth_in), BF16),
            vmem((4, SHARE, depth_out), BF16),
            vmem((64, depth_in), BF16),
            vmem((64, depth_out), BF16),
            vmem((1, 512), jnp.int32),
            vmem((1, 512), jnp.int32),
            vmem((3, SHARE, 128), BF16),
            vmem((SHARE, 128), F32),
            vmem((3, SHARE, 128), BF16),
            vmem((64, SHARE), F32),
            vmem((SLOTS, SHARE), F32),
            vmem((4, 512, 512), BF16),
            vmem((512, 2 * SHARE), BF16),
            vmem((512, 128), BF16),
            vmem((4, 512, 128), BF16),
            vmem((4, 4, 32, 128), BF16),
            vmem((4, 32, 512), BF16),
            vmem((4, 32, 512), BF16),
            vmem((4, 1024, 128), BF16),
            vmem((4, 1024, 128), BF16),
            vmem((512, 1024), BF16),
            vmem((512, 1024), BF16),
            vmem((128, 1152), BF16),
            vmem((128, 1024), BF16),
            vmem((8, 16, 1152), BF16),
            vmem((8, 16, 1024), BF16),
            dma((2, 4)),
            dma((4,)),
            dma((2,)),
            dma((2, 3)),
            dma((2, 3)),
            dma((3,)),
            dma((3,)),
            dma,
            dma((4,)),
            dma((2, 3)),
            dma((2, 3)),
            dma((2,)),
            dma((2,)),
        ],
        compiler_params=pltpu.CompilerParams(
            collective_id=0, has_side_effects=True, vmem_limit_bytes=48 * 1024 * 1024
        ),
    )(
        on_hbm(activations),
        on_hbm(out_grads),
        on_hbm(proj_in.T),
        on_hbm(proj_out.T),
        on_hbm(doc_starts.reshape(1, 512)),
        on_hbm(doc_owner.reshape(1, 512)),
        on_hbm(queries),
    )


def solution(mesh):
    in_specs = (
        P("tok", "pb"),
        P("tok", "pb"),
        P("pb", None),
        P("pb", None),
        P(),
        P(),
        P("pb", "tok"),
    )
    return jax.shard_map(
        per_device, mesh=mesh, in_specs=in_specs, out_specs=P("tok", "pb"), check_vma=False
    )
```

time: 50.9 us -> 43.2 us (0.85)
  local copies, waits for them, and re-layouts: 5.58 us -> 0.66 us
  Pallas kernels: 45 us -> 42.5 us
    unnamed x9 -> x1, local copies, waits for them, and re-layouts: 5.58 us -> 0.66 us
    pallas_call x1, Pallas kernels: 45 us -> 42.5 us  [per_device(): pl.pallas_call(kernel, out_shape=jax.ShapeDtypeStruct((16, 2048), F32), i...]
where the time goes in v2:
time: 43.2 us; the launch traced here: 43.1 us
  Pallas kernels  42.5 us (98%)
  local copies, waits for them, and re-layouts  0.66 us (2%)
    pallas_call x1, Pallas kernels, per_device(): pl.pallas_call(kernel, out_shape=jax.ShapeDtypeStruct((16, 2048), F32), i...  42.5 us

profile of v2, /device:TPU:1, one launch (start us, length us, event | category | flops | bytes accessed | tf_op | source)
XLA Modules:
  0.0 43.1 jit_solution(15851934490161390883)
XLA Ops:
  0.0 42.5 %shard_map.73 = f32[16,2048]{1,0:T(8,128)S(1)} custom-call(bf16[2048,3584]{1,0:T(8,128)(2,1)} %act_hbm.1, bf16[2048,1024]{1,0:T(8,128)(2,1)} %grad_hbm.1, bf16[64,3584]{1,0:T(8,128)(2,1)} %bitcast.4, bf16[64,1024]{1,0:T(8,128)(2,1)} %bitcast.5, s32[1,512]{1,0:T(1,128)} %bitcast.6, s32[1,512]{1,0:T(1,128)} %bitcast.7, bf16[2048,128]{1,0:T(8,128)(2,1)} %q_hbm.1), custom_call_target="tpu_custom_call" | custom-call | tf_op jit(solution)/shard_map/pallas_call | solution.py:352
  42.5 0.7 %copy.9 = f32[16,2048]{1,0:T(8,128)} copy(f32[16,2048]{1,0:T(8,128)S(1)} %shard_map.73) | data formatting | bytes 262144

commit v3 on v2

--- a/solution.py
+++ b/solution.py
@@ -12,6 +12,7 @@
 SLOTS = 16
 MESH = pl.DeviceIdType.MESH
 DEVICES = 128
+HALF = 256
 NT = (((1,), (1,)), ((), ()))
 F32 = jnp.float32
 BF16 = jnp.bfloat16
@@ -54,6 +55,7 @@
     onehot_ref,
     place,
     lhs,
+    rhs,
     wnd,
     wnd_recv,
     units,
@@ -86,13 +88,21 @@
     z, y, c = tok // 8, (tok // 2) % 4, tok % 2
     me = tok * 4 + pb
 
-    def tile_loads(t):
-        rows = pl.ds(pl.multiple_of(((pb + hop_of(t)) % 4) * SHARE, SHARE), SHARE)
+    def loads_of(rows, t, at, sem):
         return [
-            pltpu.make_async_copy(grad_hbm.at[rows], grad_buf.at[t], load_sem.at[0, t]),
-            pltpu.make_async_copy(act_hbm.at[rows], act_buf.at[t], load_sem.at[1, t]),
+            pltpu.make_async_copy(grad_hbm.at[rows], grad_buf.at[t, at], load_sem.at[0, sem]),
+            pltpu.make_async_copy(act_hbm.at[rows], act_buf.at[t, at], load_sem.at[1, sem]),
         ]
 
+    def half_of(s):
+        return lax.rem(s, 3), pl.ds(pl.multiple_of(lax.div(s, 3) * HALF, HALF), HALF)
+
+    def half_loads(s):
+        t, at = half_of(s)
+        start = lax.rem(pb + hop_of(t), 4) * SHARE + lax.div(s, 3) * HALF
+        return loads_of(pl.ds(pl.multiple_of(start, HALF), HALF), t, at, s)
+
+    own_loads = loads_of(pl.ds(pl.multiple_of(pb * SHARE, SHARE), SHARE), 3, pl.ds(0, SHARE), 6)
     small = [
         pltpu.make_async_copy(wout_hbm, wout, w_sem.at[0]),
         pltpu.make_async_copy(win_hbm, win, w_sem.at[1]),
@@ -105,7 +115,15 @@
     ]
     small[0].start()
     small[1].start()
-    for copy in q_loads + tile_loads(0) + tile_loads(1):
+    for copy in half_loads(0) + q_loads:
+        copy.start()
+
+    @pl.loop(1, 6)
+    def _(s):
+        for copy in half_loads(s):
+            copy.start()
+
+    for copy in own_loads:
         copy.start()
     small[2].start()
     small[3].start()
@@ -122,52 +140,61 @@
         for plane in planes:
             pl.semaphore_signal(barrier, inc=1, device_id=(to, plane), device_id_type=MESH)
 
-    q_copies = []
-    for n in range(1, 4):
-        to_y = z * 8 + ((y + n) % 4) * 2 + c
-        to_z = ((z + n) % 4) * 8 + y * 2 + c
-        q_copies.append(remote(qa.at[y], qa.at[y], qs_send.at[0, n - 1], qs_recv.at[0, n - 1], to_y, pb))
-        q_copies.append(remote(qb.at[z], qb.at[z], qs_send.at[1, n - 1], qs_recv.at[1, n - 1], to_z, pb))
-
-    pl.semaphore_wait(barrier, DEVICES - 1)
-    for copy in q_loads:
-        copy.wait()
-    for copy in q_copies:
-        copy.start()
+    q_copies, q_passed = [], []
+    for h, (q_all, place_me) in enumerate(((qa, y), (qb, z))):
+        right, left = lax.rem(place_me + 1, 4), lax.rem(place_me + 3, 4)
+        for k, (to, rows, src) in enumerate(
+            (
+                (right, pl.ds(0, 1024), place_me),
+                (left, pl.ds(0, 1024), place_me),
+                (right, pl.ds(0, 512), left),
+                (left, pl.ds(512, 512), right),
+            )
+        ):
+            part = q_all.at[src, rows]
+            to_tok = z * 8 + to * 2 + c if h == 0 else to * 8 + y * 2 + c
+            copy = remote(part, part, qs_send.at[h, k], qs_recv.at[h, k], to_tok, pb)
+            (q_copies if k < 2 else q_passed).append(copy)
 
     for copy in small[:2]:
         copy.wait()
 
-    def proj_copy(t):
-        return remote(
-            proj_send.at[t], proj_recv.at[t], p_send.at[t], p_recv.at[t], tok, (pb + hop_of(t)) % 4
-        )
-
-    @pl.loop(0, 4)
-    def _(t):
-        @pl.when(t < 2)
-        def _():
-            for copy in tile_loads(t + 2):
-                copy.start()
-
-        for copy in tile_loads(t):
-            copy.wait()
-        both = jnp.concatenate(
+    def project(t, at):
+        return jnp.concatenate(
             [
-                lax.dot_general(act_buf[t], win[...], NT, preferred_element_type=F32),
-                lax.dot_general(grad_buf[t], wout[...], NT, preferred_element_type=F32),
+                lax.dot_general(act_buf[t, at, :], win[...], NT, preferred_element_type=F32),
+                lax.dot_general(grad_buf[t, at, :], wout[...], NT, preferred_element_type=F32),
             ],
             axis=1,
         )
 
-        @pl.when(t < 3)
+    def proj_copy(s):
+        t, at = half_of(s)
+        return remote(
+            proj_send.at[t, at], proj_recv.at[t, at], p_send.at[s], p_recv.at[s], tok, lax.rem(pb + hop_of(t), 4)
+        )
+
+    @pl.loop(0, 6)
+    def _(s):
+        for copy in half_loads(s):
+            copy.wait()
+        t, at = half_of(s)
+        proj_send[t, at, :] = project(t, at).astype(BF16)
+
+        @pl.when(s == 0)
         def _():
-            proj_send[t] = both.astype(BF16)
-            proj_copy(t).start()
-
-        @pl.when(t == 3)
-        def _():
-            proj_own[...] = both
+            pl.semaphore_wait(barrier, DEVICES - 1)
+            for copy in q_loads:
+                copy.wait()
+            for copy in q_copies:
+                copy.start()
+
+        proj_copy(s).start()
+
+    for copy in own_loads:
+        copy.wait()
+    proj_own[...] = project(3, pl.ds(0, SHARE))
+    proj_copies = [proj_copy(s) for s in range(6)]
 
     for copy in small[2:]:
         copy.wait()
@@ -181,8 +208,8 @@
         (enters - leaves).astype(BF16), begun.astype(F32).astype(BF16), NT, preferred_element_type=F32
     )
 
-    for t in range(3):
-        proj_copy(t).wait_recv()
+    for copy in proj_copies:
+        copy.wait_recv()
     proj = proj_own[...]
     for t in range(3):
         proj = proj + proj_recv[t].astype(F32)
@@ -190,16 +217,12 @@
 
     proj_t[...] = proj.T[64:128, :]
     onehot = onehot_ref[...]
-    for r in range(64):
-        picked = onehot * proj_t[r : r + 1, :]
-        lhs[pl.ds((r // 2) * SLOTS, SLOTS), pl.ds((r % 2) * SHARE, SHARE)] = picked.astype(BF16)
     low = lax.broadcasted_iota(jnp.int32, (SHARE, 128), 1) < 64
-    rhs = jnp.concatenate(
+    rhs[...] = jnp.concatenate(
         [jnp.where(low, proj, 0.0), jnp.where(low, 0.0, pltpu.roll(proj, 64, 1))], axis=0
     ).astype(BF16)
-    wnd[...] = jnp.dot(lhs[...], rhs, preferred_element_type=F32).astype(BF16)
-
-    mine = pl.ds(pl.multiple_of((me % 32) * SLOTS, SLOTS), SLOTS)
+    mine = pl.ds(pl.multiple_of(lax.rem(me, 32) * SLOTS, SLOTS), SLOTS)
+    far_planes = [planes[2], planes[1], planes[3], planes[0]]
 
     def send_block(to, plane):
         remote(
@@ -211,16 +234,38 @@
             plane,
         ).start()
 
-    for plane in planes[1:]:
-        send_block(tok, plane)
-
-    @pl.loop(1, 32)
-    def _(n):
-        to = lax.rem(tok + n, 32)
-        for plane in planes:
-            send_block(to, plane)
+    @pl.loop(0, 4)
+    def _(k):
+        g = lax.rem(z + hop_of(k), 4)
+        rows = proj_t[pl.ds(pl.multiple_of(g * 16, 16), 16), :]
+        for r in range(16):
+            picked = onehot * rows[r : r + 1, :]
+            lhs[pl.ds((r // 2) * SLOTS, SLOTS), pl.ds((r % 2) * SHARE, SHARE)] = picked.astype(BF16)
+        wnd[pl.ds(pl.multiple_of(g * 128, 128), 128), :] = jnp.dot(
+            lhs[...], rhs[...], preferred_element_type=F32
+        ).astype(BF16)
+
+        @pl.loop(0, 3)
+        def _(n):
+            row = g * 8 + lax.rem(y + hop_of(n), 4) * 2
+            for plane in far_planes:
+                send_block(row + c, plane)
+                send_block(row + 1 - c, plane)
+
+        for plane in far_planes[:3]:
+            send_block(g * 8 + y * 2 + c, plane)
+            send_block(g * 8 + y * 2 + 1 - c, plane)
+        send_block(g * 8 + y * 2 + 1 - c, pb)
+
+        @pl.when(k < 3)
+        def _():
+            send_block(g * 8 + y * 2 + c, pb)
 
     wnd_recv[z, mine, :] = wnd[pl.ds(pl.multiple_of(tok * SLOTS, SLOTS), SLOTS), :]
+    for copy in q_copies:
+        copy.wait_recv()
+    for copy in q_passed:
+        copy.start()
 
     lane8 = lax.broadcasted_iota(jnp.int32, (8, 512), 1)
     row8 = lax.broadcasted_iota(jnp.int32, (8, 512), 0)
@@ -241,14 +286,8 @@
         inside = (from_block <= block) & (block <= to_block) & own_slot
         place[g] = inside.astype(F32).astype(BF16)
 
-    for copy in q_copies:
-        copy.wait_recv()
-    for n in range(4):
-        qa_t[pl.ds(n * 128, 128), :] = qa[n].T
-        qb_t[pl.ds(n * 128, 128), :] = qb[n].T
-
     summed = jnp.zeros((512, 128), F32)
-    for n in (3, 2, 1, 0):
+    for n in (2, 3, 1, 0):
         g = (z + n) % 4
         got = wnd_recv.at[g, pl.ds(0, 512 if n else 496)]
         pltpu.make_async_copy(got, got, d_recv.at[g]).wait()
@@ -276,6 +315,12 @@
     vb[:, :, at_z] = units[z]
     fa_me, fb_me = z * 2 + c, y * 2 + c
 
+    for copy in q_passed:
+        copy.wait_recv()
+    for n in range(4):
+        qa_t[pl.ds(n * 128, 128), :] = qa[n].T
+        qb_t[pl.ds(n * 128, 128), :] = qb[n].T
+
     for copy in u_copies[0::2]:
         copy.wait_recv()
     fb[...] = jnp.dot(vb[...].reshape(128, 512), qb_t[...], preferred_element_type=F32).astype(BF16)
@@ -330,9 +375,7 @@
     out_ref[:, :1024] = total_a[:, :1024] * norm
     out_ref[:, 1024:] = total_b * norm
 
-    for t in range(3):
-        proj_copy(t).wait_send()
-    for copy in q_copies + u_copies:
+    for copy in proj_copies + q_copies + q_passed + u_copies:
         copy.wait_send()
     for g in range(4):
         some = wnd.at[pl.ds(0, 512 if g else 496)]
@@ -367,7 +410,8 @@
             vmem((64, SHARE), F32),
             vmem((SLOTS, SHARE), F32),
             vmem((4, 512, 512), BF16),
-            vmem((512, 2 * SHARE), BF16),
+            vmem((128, 2 * SHARE), BF16),
+            vmem((2 * SHARE, 128), BF16),
             vmem((512, 128), BF16),
             vmem((4, 512, 128), BF16),
             vmem((4, 4, 32, 128), BF16),
@@ -381,13 +425,13 @@
             vmem((128, 1024), BF16),
             vmem((8, 16, 1152), BF16),
             vmem((8, 16, 1024), BF16),
-            dma((2, 4)),
+            dma((2, 7)),
             dma((4,)),
             dma((2,)),
-            dma((2, 3)),
-            dma((2, 3)),
-            dma((3,)),
-            dma((3,)),
+            dma((2, 4)),
+            dma((2, 4)),
+            dma((6,)),
+            dma((6,)),
             dma,
             dma((4,)),
             dma((2, 3)),

time: 43.2 us -> 40.8 us (0.944)
  Pallas kernels: 42.5 us -> 40 us
    pallas_call x1, Pallas kernels: 42.5 us -> 40 us  [per_device(): pl.pallas_call(kernel, out_shape=jax.ShapeDtypeStruct((16, 2048), F32), i...]
where the time goes in v3:
time: 40.8 us; the launch traced here: 40.7 us
  Pallas kernels  40 us (98%)
  local copies, waits for them, and re-layouts  0.66 us (2%)
    pallas_call x1, Pallas kernels, per_device(): pl.pallas_call(kernel, out_shape=jax.ShapeDtypeStruct((16, 2048), F32), i...  40 us

profile of v3, /device:TPU:1, one launch (start us, length us, event | category | flops | bytes accessed | tf_op | source)
XLA Modules:
  0.0 40.7 jit_solution(3155994092979803340)
XLA Ops:
  0.0 40.0 %shard_map.73 = f32[16,2048]{1,0:T(8,128)S(1)} custom-call(bf16[2048,3584]{1,0:T(8,128)(2,1)} %act_hbm.1, bf16[2048,1024]{1,0:T(8,128)(2,1)} %grad_hbm.1, bf16[64,3584]{1,0:T(8,128)(2,1)} %bitcast.4, bf16[64,1024]{1,0:T(8,128)(2,1)} %bitcast.5, s32[1,512]{1,0:T(1,128)} %bitcast.6, s32[1,512]{1,0:T(1,128)} %bitcast.7, bf16[2048,128]{1,0:T(8,128)(2,1)} %q_hbm.1), custom_call_target="tpu_custom_call" | custom-call | tf_op jit(solution)/shard_map/pallas_call | solution.py:395
  40.0 0.7 %copy.9 = f32[16,2048]{1,0:T(8,128)} copy(f32[16,2048]{1,0:T(8,128)S(1)} %shard_map.73) | data formatting | bytes 262144

commit v4 on v3

--- a/solution.py
+++ b/solution.py
@@ -9,7 +9,9 @@
 
 EPS = 1e-06
 SHARE = 512
-SLOTS = 16
+SLOTS = 10
+PAIRS = SLOTS // 2
+GROUP = 8 * SLOTS
 MESH = pl.DeviceIdType.MESH
 DEVICES = 128
 HALF = 256
@@ -27,6 +29,11 @@
         device_id=(tok, pb),
         device_id_type=MESH,
     )
+
+
+def split_slots(numbers):
+    quotient = jnp.floor((numbers + 0.5) * (1.0 / SLOTS))
+    return quotient, numbers - SLOTS * quotient
 
 
 def hop_of(t):
@@ -51,7 +58,7 @@
     proj_send,
     proj_own,
     proj_recv,
-    proj_t,
+    proj_relay,
     onehot_ref,
     place,
     lhs,
@@ -95,11 +102,13 @@
         ]
 
     def half_of(s):
-        return lax.rem(s, 3), pl.ds(pl.multiple_of(lax.div(s, 3) * HALF, HALF), HALF)
+        t = jnp.where(s < 2, 0, 1 + lax.rem(s, 2))
+        h = jnp.where((s == 0) | (s == 3) | (s == 4), 0, 1)
+        return t, pl.ds(pl.multiple_of(h * HALF, HALF), HALF), h
 
     def half_loads(s):
-        t, at = half_of(s)
-        start = lax.rem(pb + hop_of(t), 4) * SHARE + lax.div(s, 3) * HALF
+        t, at, h = half_of(s)
+        start = lax.rem(pb + hop_of(t), 4) * SHARE + h * HALF
         return loads_of(pl.ds(pl.multiple_of(start, HALF), HALF), t, at, s)
 
     own_loads = loads_of(pl.ds(pl.multiple_of(pb * SHARE, SHARE), SHARE), 3, pl.ds(0, SHARE), 6)
@@ -140,21 +149,23 @@
         for plane in planes:
             pl.semaphore_signal(barrier, inc=1, device_id=(to, plane), device_id_type=MESH)
 
-    q_copies, q_passed = [], []
+    q_first, q_second, q_passed = [], [], []
     for h, (q_all, place_me) in enumerate(((qa, y), (qb, z))):
         right, left = lax.rem(place_me + 1, 4), lax.rem(place_me + 3, 4)
-        for k, (to, rows, src) in enumerate(
+        for k, (to, row, src, group) in enumerate(
             (
-                (right, pl.ds(0, 1024), place_me),
-                (left, pl.ds(0, 1024), place_me),
-                (right, pl.ds(0, 512), left),
-                (left, pl.ds(512, 512), right),
+                (right, 0, place_me, q_first),
+                (left, 512, place_me, q_first),
+                (right, 512, place_me, q_second),
+                (left, 0, place_me, q_second),
+                (right, 0, left, q_passed),
+                (left, 512, right, q_passed),
             )
         ):
-            part = q_all.at[src, rows]
+            part = q_all.at[src, pl.ds(row, 512)]
             to_tok = z * 8 + to * 2 + c if h == 0 else to * 8 + y * 2 + c
-            copy = remote(part, part, qs_send.at[h, k], qs_recv.at[h, k], to_tok, pb)
-            (q_copies if k < 2 else q_passed).append(copy)
+            group.append(remote(part, part, qs_send.at[h, k], qs_recv.at[h, k], to_tok, pb))
+    q_copies = q_first + q_second + q_passed
 
     for copy in small[:2]:
         copy.wait()
@@ -168,65 +179,98 @@
             axis=1,
         )
 
+    def relay_copy(s):
+        return remote(
+            proj_send.at[0, half_of(s)[1]],
+            proj_relay.at[s],
+            p_send.at[s],
+            p_recv.at[s],
+            tok,
+            lax.rem(pb + 1 + 2 * s, 4),
+        )
+
     def proj_copy(s):
-        t, at = half_of(s)
+        t, at, _ = half_of(s)
         return remote(
-            proj_send.at[t, at], proj_recv.at[t, at], p_send.at[s], p_recv.at[s], tok, lax.rem(pb + hop_of(t), 4)
+            proj_send.at[t, at], proj_recv.at[t - 1, at], p_send.at[s], p_recv.at[s], tok, lax.rem(pb + hop_of(t), 4)
         )
 
     @pl.loop(0, 6)
     def _(s):
         for copy in half_loads(s):
             copy.wait()
-        t, at = half_of(s)
-        proj_send[t, at, :] = project(t, at).astype(BF16)
+        t, at, _ = half_of(s)
+        both = project(t, at)
+
+        @pl.when(s < 4)
+        def _():
+            proj_send[t, at, :] = both.astype(BF16)
 
         @pl.when(s == 0)
         def _():
             pl.semaphore_wait(barrier, DEVICES - 1)
             for copy in q_loads:
                 copy.wait()
-            for copy in q_copies:
+            for copy in q_first + q_second:
                 copy.start()
 
-        proj_copy(s).start()
+        @pl.when(s < 2)
+        def _():
+            relay_copy(s).start()
+
+        @pl.when(s >= 4)
+        def _():
+            relay_copy(s - 4).wait_recv()
+            proj_send[t, at, :] = (both + proj_relay[s - 4].astype(F32)).astype(BF16)
+
+        @pl.when(s >= 2)
+        def _():
+            proj_copy(s).start()
 
     for copy in own_loads:
         copy.wait()
     proj_own[...] = project(3, pl.ds(0, SHARE))
-    proj_copies = [proj_copy(s) for s in range(6)]
+    for copy in q_first:
+        copy.wait_recv()
+    for copy in q_passed:
+        copy.start()
+    relay_copies = [relay_copy(s) for s in range(2)]
+    proj_copies = [proj_copy(s) for s in range(2, 6)]
 
     for copy in small[2:]:
         copy.wait()
     starts = starts_ref[...]
     begun = starts <= me * SHARE + lax.broadcasted_iota(jnp.int32, (SHARE, 512), 0)
-    doc_lane = lax.broadcasted_iota(jnp.int32, (SLOTS, 512), 1)
-    slot_row = lax.broadcasted_iota(jnp.int32, (SLOTS, 512), 0)
-    enters = (doc_lane % SLOTS == slot_row).astype(F32)
-    leaves = ((doc_lane > 0) & ((doc_lane + SLOTS - 1) % SLOTS == slot_row)).astype(F32)
+    doc = lax.broadcasted_iota(jnp.int32, (8, 512), 1).astype(F32)
+    doc_slot = split_slots(doc)[1]
+    slot_before = jnp.where(doc > 0, split_slots(doc - 1)[1], -1.0)
+    row_block, row_slot = split_slots(lax.broadcasted_iota(jnp.int32, (GROUP, 128), 0).astype(F32))
+    slot_row = row_slot[:, 0:1]
+    enters = (doc_slot[0:1, :] == slot_row).astype(F32) - (slot_before[0:1, :] == slot_row).astype(F32)
     onehot_ref[...] = lax.dot_general(
-        (enters - leaves).astype(BF16), begun.astype(F32).astype(BF16), NT, preferred_element_type=F32
+        enters.astype(BF16), begun.astype(F32).astype(BF16), NT, preferred_element_type=F32
     )
 
     for copy in proj_copies:
         copy.wait_recv()
     proj = proj_own[...]
-    for t in range(3):
+    for t in range(2):
         proj = proj + proj_recv[t].astype(F32)
-    proj = proj.astype(BF16).astype(F32)
-
-    proj_t[...] = proj.T[64:128, :]
+    proj = proj.astype(BF16)
+
     onehot = onehot_ref[...]
+    lane = lax.broadcasted_iota(jnp.int32, (GROUP, 128), 1)
     low = lax.broadcasted_iota(jnp.int32, (SHARE, 128), 1) < 64
+    wide = proj.astype(F32)
     rhs[...] = jnp.concatenate(
-        [jnp.where(low, proj, 0.0), jnp.where(low, 0.0, pltpu.roll(proj, 64, 1))], axis=0
+        [jnp.where(low, wide, 0.0), jnp.where(low, 0.0, pltpu.roll(wide, 64, 1))], axis=0
     ).astype(BF16)
-    mine = pl.ds(pl.multiple_of(lax.rem(me, 32) * SLOTS, SLOTS), SLOTS)
+    mine = pl.ds(lax.rem(me, 32) * PAIRS, PAIRS)
     far_planes = [planes[2], planes[1], planes[3], planes[0]]
 
     def send_block(to, plane):
         remote(
-            wnd.at[pl.ds(pl.multiple_of(to * SLOTS, SLOTS), SLOTS)],
+            wnd.at[pl.ds(to * PAIRS, PAIRS)],
             wnd_recv.at[z, mine],
             d_send,
             d_recv.at[z],
@@ -237,13 +281,13 @@
     @pl.loop(0, 4)
     def _(k):
         g = lax.rem(z + hop_of(k), 4)
-        rows = proj_t[pl.ds(pl.multiple_of(g * 16, 16), 16), :]
-        for r in range(16):
-            picked = onehot * rows[r : r + 1, :]
-            lhs[pl.ds((r // 2) * SLOTS, SLOTS), pl.ds((r % 2) * SHARE, SHARE)] = picked.astype(BF16)
-        wnd[pl.ds(pl.multiple_of(g * 128, 128), 128), :] = jnp.dot(
-            lhs[...], rhs[...], preferred_element_type=F32
-        ).astype(BF16)
+        first_r = (64 + g * 16).astype(F32) + 2 * row_block
+        for half in range(2):
+            pick = (lane.astype(F32) == first_r + half).astype(F32).astype(BF16)
+            of_row = lax.dot_general(pick, proj, NT, preferred_element_type=F32)
+            lhs[:, pl.ds(half * SHARE, SHARE)] = (onehot * of_row).astype(BF16)
+        sums = jnp.dot(lhs[...], rhs[...], preferred_element_type=F32)
+        wnd[pl.ds(g * 8 * PAIRS, 8 * PAIRS)] = sums.astype(BF16).reshape(8 * PAIRS, 2, 128)
 
         @pl.loop(0, 3)
         def _(n):
@@ -261,23 +305,18 @@
         def _():
             send_block(g * 8 + y * 2 + c, pb)
 
-    wnd_recv[z, mine, :] = wnd[pl.ds(pl.multiple_of(tok * SLOTS, SLOTS), SLOTS), :]
-    for copy in q_copies:
-        copy.wait_recv()
-    for copy in q_passed:
-        copy.start()
-
+    wnd_recv[z, mine] = wnd[pl.ds(tok * PAIRS, PAIRS)]
     lane8 = lax.broadcasted_iota(jnp.int32, (8, 512), 1)
     row8 = lax.broadcasted_iota(jnp.int32, (8, 512), 0)
     first = jnp.broadcast_to(starts, (8, 512)) // SHARE
     last = jnp.where(lane8 == 511, DEVICES - 1, pltpu.roll(first, 511, 1))
-    facts = jnp.where(row8 == 0, first, jnp.where(row8 == 1, last, lane8 % SLOTS))
+    facts = jnp.where(row8 == 0, first.astype(F32), jnp.where(row8 == 1, last.astype(F32), doc_slot))
     rank = owner_ref[...] * 16 + lax.broadcasted_iota(jnp.int32, (1, 512), 1) // 32
     perm = (rank == lax.broadcasted_iota(jnp.int32, (512, 512), 0)).astype(F32).astype(BF16)
-    ranked = lax.dot_general(perm, facts.astype(F32).astype(BF16), NT, preferred_element_type=F32)
-    col = lax.broadcasted_iota(jnp.int32, (512, 512), 1)
-    block = (col // SLOTS).astype(F32)
-    own_slot = ranked[:, 2:3] == (col % SLOTS).astype(F32)
+    ranked = lax.dot_general(perm, facts.astype(BF16), NT, preferred_element_type=F32)
+    block, slot = split_slots(lax.broadcasted_iota(jnp.int32, (8, 32 * SLOTS), 1).astype(F32))
+    block = block[0:1, :]
+    own_slot = ranked[:, 2:3] == slot[0:1, :]
 
     @pl.loop(0, 4)
     def _(g):
@@ -289,9 +328,11 @@
     summed = jnp.zeros((512, 128), F32)
     for n in (2, 3, 1, 0):
         g = (z + n) % 4
-        got = wnd_recv.at[g, pl.ds(0, 512 if n else 496)]
+        got = wnd_recv.at[g, pl.ds(0, (32 if n else 31) * PAIRS)]
         pltpu.make_async_copy(got, got, d_recv.at[g]).wait()
-        summed = summed + jnp.dot(place[g], wnd_recv[g], preferred_element_type=F32)
+        summed = summed + jnp.dot(
+            place[g], wnd_recv[g].reshape(32 * SLOTS, 128), preferred_element_type=F32
+        )
     units[...] = summed.astype(BF16).reshape(4, 4, 32, 128)
 
     at_y = pl.ds(pl.multiple_of(y * 128, 128), 128)
@@ -315,7 +356,7 @@
     vb[:, :, at_z] = units[z]
     fa_me, fb_me = z * 2 + c, y * 2 + c
 
-    for copy in q_passed:
+    for copy in q_second + q_passed:
         copy.wait_recv()
     for n in range(4):
         qa_t[pl.ds(n * 128, 128), :] = qa[n].T
@@ -375,10 +416,10 @@
     out_ref[:, :1024] = total_a[:, :1024] * norm
     out_ref[:, 1024:] = total_b * norm
 
-    for copy in proj_copies + q_copies + q_passed + u_copies:
+    for copy in relay_copies + proj_copies + q_copies + u_copies:
         copy.wait_send()
     for g in range(4):
-        some = wnd.at[pl.ds(0, 512 if g else 496)]
+        some = wnd.at[pl.ds(0, (32 if g else 31) * PAIRS)]
         pltpu.make_async_copy(some, some, d_send).wait()
     pltpu.make_async_copy(fa.at[pl.ds(0, 112)], fa.at[pl.ds(0, 112)], f_send.at[0]).wait()
     pltpu.make_async_copy(fb.at[pl.ds(0, 112)], fb.at[pl.ds(0, 112)], f_send.at[1]).wait()
@@ -406,14 +447,14 @@
             vmem((1, 512), jnp.int32),
             vmem((3, SHARE, 128), BF16),
             vmem((SHARE, 128), F32),
-            vmem((3, SHARE, 128), BF16),
-            vmem((64, SHARE), F32),
-            vmem((SLOTS, SHARE), F32),
-            vmem((4, 512, 512), BF16),
-            vmem((128, 2 * SHARE), BF16),
+            vmem((2, SHARE, 128), BF16),
+            vmem((2, HALF, 128), BF16),
+            vmem((GROUP, SHARE), F32),
+            vmem((4, 512, 32 * SLOTS), BF16),
+            vmem((GROUP, 2 * SHARE), BF16),
             vmem((2 * SHARE, 128), BF16),
-            vmem((512, 128), BF16),
-            vmem((4, 512, 128), BF16),
+            vmem((32 * PAIRS, 2, 128), BF16),
+            vmem((4, 32 * PAIRS, 2, 128), BF16),
             vmem((4, 4, 32, 128), BF16),
             vmem((4, 32, 512), BF16),
             vmem((4, 32, 512), BF16),
@@ -428,8 +469,8 @@
             dma((2, 7)),
             dma((4,)),
             dma((2,)),
-            dma((2, 4)),
-            dma((2, 4)),
+            dma((2, 6)),
+            dma((2, 6)),
             dma((6,)),
             dma((6,)),
             dma,

time: 40.8 us -> 38.4 us (0.941)
  Pallas kernels: 40 us -> 37.6 us
    pallas_call x1, Pallas kernels: 40 us -> 37.6 us  [per_device(): pl.pallas_call(kernel, out_shape=jax.ShapeDtypeStruct((16, 2048), F32), i...]
where the time goes in v4:
time: 38.4 us; the launch traced here: 38.3 us
  Pallas kernels  37.6 us (98%)
  local copies, waits for them, and re-layouts  0.66 us (2%)
    pallas_call x1, Pallas kernels, per_device(): pl.pallas_call(kernel, out_shape=jax.ShapeDtypeStruct((16, 2048), F32), i...  37.6 us

profile of v4, /device:TPU:1, one launch (start us, length us, event | category | flops | bytes accessed | tf_op | source)
XLA Modules:
  0.0 38.3 jit_solution(7184484628852778267)
XLA Ops:
  0.0 37.6 %shard_map.73 = f32[16,2048]{1,0:T(8,128)S(1)} custom-call(bf16[2048,3584]{1,0:T(8,128)(2,1)} %act_hbm.1, bf16[2048,1024]{1,0:T(8,128)(2,1)} %grad_hbm.1, bf16[64,3584]{1,0:T(8,128)(2,1)} %bitcast.4, bf16[64,1024]{1,0:T(8,128)(2,1)} %bitcast.5, s32[1,512]{1,0:T(1,128)} %bitcast.6, s32[1,512]{1,0:T(1,128)} %bitcast.7, bf16[2048,128]{1,0:T(8,128)(2,1)} %q_hbm.1), custom_call_target="tpu_custom_call" | custom-call | tf_op jit(solution)/shard_map/pallas_call | solution.py:436
  37.6 0.7 %copy.9 = f32[16,2048]{1,0:T(8,128)} copy(f32[16,2048]{1,0:T(8,128)S(1)} %shard_map.73) | data formatting | bytes 262144

commit v5 on v4

--- a/solution.py
+++ b/solution.py
@@ -89,6 +89,7 @@
     u_recv,
     f_send,
     f_recv,
+    round_sem,
 ):
     tok = lax.axis_index("tok")
     pb = lax.axis_index("pb")
@@ -137,17 +138,19 @@
     small[2].start()
     small[3].start()
 
+    planes = [lax.rem(pb + n, 4) for n in range(4)]
+    on_y = [z * 8 + lax.rem(y + n, 4) * 2 + c for n in range(1, 4)]
+    on_z = [lax.rem(z + n, 4) * 8 + y * 2 + c for n in range(1, 4)]
+    on_core = [z * 8 + y * 2 + 1 - c]
+
+    def signal(sem, toks):
+        for to in toks:
+            pl.semaphore_signal(sem, inc=1, device_id=(to, pb), device_id_type=MESH)
+
     barrier = pltpu.get_barrier_semaphore()
-
-    planes = [lax.rem(pb + n, 4) for n in range(4)]
     for plane in planes[1:]:
         pl.semaphore_signal(barrier, inc=1, device_id=(tok, plane), device_id_type=MESH)
-
-    @pl.loop(1, 32)
-    def _(n):
-        to = lax.rem(tok + n, 32)
-        for plane in planes:
-            pl.semaphore_signal(barrier, inc=1, device_id=(to, plane), device_id_type=MESH)
+    signal(barrier, on_y + on_z + on_core)
 
     q_first, q_second, q_passed = [], [], []
     for h, (q_all, place_me) in enumerate(((qa, y), (qb, z))):
@@ -208,7 +211,8 @@
 
         @pl.when(s == 0)
         def _():
-            pl.semaphore_wait(barrier, DEVICES - 1)
+            pl.semaphore_wait(barrier, 10)
+            signal(round_sem.at[0], on_y)
             for copy in q_loads:
                 copy.wait()
             for copy in q_first + q_second:
@@ -218,6 +222,16 @@
         def _():
             relay_copy(s).start()
 
+        @pl.when(s == 2)
+        def _():
+            pl.semaphore_wait(round_sem.at[0], 3)
+            signal(round_sem.at[1], on_z)
+
+        @pl.when(s == 4)
+        def _():
+            pl.semaphore_wait(round_sem.at[1], 3)
+            signal(round_sem.at[2], on_core)
+
         @pl.when(s >= 4)
         def _():
             relay_copy(s - 4).wait_recv()
@@ -230,6 +244,7 @@
     for copy in own_loads:
         copy.wait()
     proj_own[...] = project(3, pl.ds(0, SHARE))
+    pl.semaphore_wait(round_sem.at[2], 1)
     for copy in q_first:
         copy.wait_recv()
     for copy in q_passed:
@@ -479,6 +494,7 @@
             dma((2, 3)),
             dma((2,)),
             dma((2,)),
+            pltpu.SemaphoreType.REGULAR((3,)),
         ],
         compiler_params=pltpu.CompilerParams(
             collective_id=0, has_side_effects=True, vmem_limit_bytes=48 * 1024 * 1024

time: 38.4 us -> 36.9 us (0.961)
  Pallas kernels: 37.6 us -> 36.2 us
    pallas_call x1, Pallas kernels: 37.6 us -> 36.2 us  [per_device(): pl.pallas_call(kernel, out_shape=jax.ShapeDtypeStruct((16, 2048), F32), i...]
where the time goes in v5:
time: 36.9 us; the launch traced here: 36.8 us
  Pallas kernels  36.2 us (98%)
  local copies, waits for them, and re-layouts  0.66 us (2%)
    pallas_call x1, Pallas kernels, per_device(): pl.pallas_call(kernel, out_shape=jax.ShapeDtypeStruct((16, 2048), F32), i...  36.2 us

profile of v5, /device:TPU:1, one launch (start us, length us, event | category | flops | bytes accessed | tf_op | source)
XLA Modules:
  0.0 36.8 jit_solution(17586137438043495226)
XLA Ops:
  0.0 36.2 %shard_map.73 = f32[16,2048]{1,0:T(8,128)S(1)} custom-call(bf16[2048,3584]{1,0:T(8,128)(2,1)} %act_hbm.1, bf16[2048,1024]{1,0:T(8,128)(2,1)} %grad_hbm.1, bf16[64,3584]{1,0:T(8,128)(2,1)} %bitcast.4, bf16[64,1024]{1,0:T(8,128)(2,1)} %bitcast.5, s32[1,512]{1,0:T(1,128)} %bitcast.6, s32[1,512]{1,0:T(1,128)} %bitcast.7, bf16[2048,128]{1,0:T(8,128)(2,1)} %q_hbm.1), custom_call_target="tpu_custom_call" | custom-call | tf_op jit(solution)/shard_map/pallas_call | solution.py:451
  36.2 0.7 %copy.9 = f32[16,2048]{1,0:T(8,128)} copy(f32[16,2048]{1,0:T(8,128)S(1)} %shard_map.73) | data formatting | bytes 262144

commit v6 on v5

--- a/solution.py
+++ b/solution.py
@@ -31,6 +31,10 @@
     )
 
 
+def drain(ref, sem):
+    pltpu.make_async_copy(ref, ref, sem).wait()
+
+
 def split_slots(numbers):
     quotient = jnp.floor((numbers + 0.5) * (1.0 / SLOTS))
     return quotient, numbers - SLOTS * quotient
@@ -49,12 +53,9 @@
     owner_hbm,
     q_hbm,
     out_ref,
-    act_buf,
-    grad_buf,
-    win,
-    wout,
-    starts_ref,
-    owner_ref,
+    tokens,
+    weights,
+    docs_ref,
     proj_send,
     proj_own,
     proj_recv,
@@ -68,8 +69,7 @@
     units,
     va,
     vb,
-    qa,
-    qb,
+    q_all,
     qa_t,
     qb_t,
     fa,
@@ -78,10 +78,12 @@
     fb_recv,
     load_sem,
     w_sem,
+    docs_sem,
     q_sem,
     qs_send,
     qs_recv,
     p_send,
+    relay_recv,
     p_recv,
     d_send,
     d_recv,
@@ -96,10 +98,14 @@
     z, y, c = tok // 8, (tok // 2) % 4, tok % 2
     me = tok * 4 + pb
 
+    depth_in = act_hbm.shape[1]
+    depth_out = grad_hbm.shape[1]
+    of_act, of_grad = pl.ds(0, depth_in), pl.ds(depth_in, depth_out)
+
     def loads_of(rows, t, at, sem):
         return [
-            pltpu.make_async_copy(grad_hbm.at[rows], grad_buf.at[t, at], load_sem.at[0, sem]),
-            pltpu.make_async_copy(act_hbm.at[rows], act_buf.at[t, at], load_sem.at[1, sem]),
+            pltpu.make_async_copy(grad_hbm.at[rows], tokens.at[t, at, of_grad], load_sem.at[sem]),
+            pltpu.make_async_copy(act_hbm.at[rows], tokens.at[t, at, of_act], load_sem.at[sem]),
         ]
 
     def half_of(s):
@@ -114,14 +120,14 @@
 
     own_loads = loads_of(pl.ds(pl.multiple_of(pb * SHARE, SHARE), SHARE), 3, pl.ds(0, SHARE), 6)
     small = [
-        pltpu.make_async_copy(wout_hbm, wout, w_sem.at[0]),
-        pltpu.make_async_copy(win_hbm, win, w_sem.at[1]),
-        pltpu.make_async_copy(starts_hbm, starts_ref, w_sem.at[2]),
-        pltpu.make_async_copy(owner_hbm, owner_ref, w_sem.at[3]),
+        pltpu.make_async_copy(wout_hbm, weights.at[pl.ds(64, 64), of_grad], w_sem),
+        pltpu.make_async_copy(win_hbm, weights.at[pl.ds(0, 64), of_act], w_sem),
+        pltpu.make_async_copy(starts_hbm, docs_ref.at[0], docs_sem),
+        pltpu.make_async_copy(owner_hbm, docs_ref.at[1], docs_sem),
     ]
     q_loads = [
-        pltpu.make_async_copy(q_hbm.at[pl.ds(0, 1024)], qa.at[y], q_sem.at[0]),
-        pltpu.make_async_copy(q_hbm.at[pl.ds(1024, 1024)], qb.at[z], q_sem.at[1]),
+        pltpu.make_async_copy(q_hbm.at[pl.ds(0, 1024)], q_all.at[0, y], q_sem),
+        pltpu.make_async_copy(q_hbm.at[pl.ds(1024, 1024)], q_all.at[1, z], q_sem),
     ]
     small[0].start()
     small[1].start()
@@ -153,7 +159,7 @@
     signal(barrier, on_y + on_z + on_core)
 
     q_first, q_second, q_passed = [], [], []
-    for h, (q_all, place_me) in enumerate(((qa, y), (qb, z))):
+    for h, place_me in enumerate((y, z)):
         right, left = lax.rem(place_me + 1, 4), lax.rem(place_me + 3, 4)
         for k, (to, row, src, group) in enumerate(
             (
@@ -165,29 +171,23 @@
                 (left, 512, right, q_passed),
             )
         ):
-            part = q_all.at[src, pl.ds(row, 512)]
+            part = q_all.at[h, src, pl.ds(row, 512)]
             to_tok = z * 8 + to * 2 + c if h == 0 else to * 8 + y * 2 + c
-            group.append(remote(part, part, qs_send.at[h, k], qs_recv.at[h, k], to_tok, pb))
-    q_copies = q_first + q_second + q_passed
-
-    for copy in small[:2]:
-        copy.wait()
+            group.append(remote(part, part, qs_send, qs_recv.at[0 if k < 2 else 1], to_tok, pb))
+
+    weights[:64, depth_in:] = jnp.zeros((64, depth_out), BF16)
+    weights[64:, :depth_in] = jnp.zeros((64, depth_in), BF16)
+    drain(weights.at[pl.ds(0, 64)], w_sem)
 
     def project(t, at):
-        return jnp.concatenate(
-            [
-                lax.dot_general(act_buf[t, at, :], win[...], NT, preferred_element_type=F32),
-                lax.dot_general(grad_buf[t, at, :], wout[...], NT, preferred_element_type=F32),
-            ],
-            axis=1,
-        )
+        return lax.dot_general(tokens[t, at, :], weights[...], NT, preferred_element_type=F32)
 
     def relay_copy(s):
         return remote(
             proj_send.at[0, half_of(s)[1]],
             proj_relay.at[s],
-            p_send.at[s],
-            p_recv.at[s],
+            p_send,
+            relay_recv.at[s],
             tok,
             lax.rem(pb + 1 + 2 * s, 4),
         )
@@ -195,14 +195,13 @@
     def proj_copy(s):
         t, at, _ = half_of(s)
         return remote(
-            proj_send.at[t, at], proj_recv.at[t - 1, at], p_send.at[s], p_recv.at[s], tok, lax.rem(pb + hop_of(t), 4)
+            proj_send.at[t, at], proj_recv.at[t - 1, at], p_send, p_recv, tok, lax.rem(pb + hop_of(t), 4)
         )
 
     @pl.loop(0, 6)
     def _(s):
-        for copy in half_loads(s):
-            copy.wait()
         t, at, _ = half_of(s)
+        drain(tokens.at[t, at], load_sem.at[s])
         both = project(t, at)
 
         @pl.when(s < 4)
@@ -213,10 +212,6 @@
         def _():
             pl.semaphore_wait(barrier, 10)
             signal(round_sem.at[0], on_y)
-            for copy in q_loads:
-                copy.wait()
-            for copy in q_first + q_second:
-                copy.start()
 
         @pl.when(s < 2)
         def _():
@@ -234,27 +229,33 @@
 
         @pl.when(s >= 4)
         def _():
-            relay_copy(s - 4).wait_recv()
+            drain(proj_relay.at[s - 4], relay_recv.at[s - 4])
             proj_send[t, at, :] = (both + proj_relay[s - 4].astype(F32)).astype(BF16)
 
         @pl.when(s >= 2)
         def _():
             proj_copy(s).start()
 
-    for copy in own_loads:
-        copy.wait()
+        @pl.when(s == 0)
+        def _():
+            drain(q_all.at[0, pl.ds(0, 2)], q_sem)
+            for copy in q_first:
+                copy.start()
+
+        @pl.when(s == 0)
+        def _():
+            for copy in q_second:
+                copy.start()
+
+    drain(tokens.at[3], load_sem.at[6])
     proj_own[...] = project(3, pl.ds(0, SHARE))
     pl.semaphore_wait(round_sem.at[2], 1)
-    for copy in q_first:
-        copy.wait_recv()
+    drain(q_all.at[0, pl.ds(0, 2)], qs_recv.at[0])
     for copy in q_passed:
         copy.start()
-    relay_copies = [relay_copy(s) for s in range(2)]
-    proj_copies = [proj_copy(s) for s in range(2, 6)]
-
-    for copy in small[2:]:
-        copy.wait()
-    starts = starts_ref[...]
+
+    drain(docs_ref, docs_sem)
+    starts = docs_ref[0]
     begun = starts <= me * SHARE + lax.broadcasted_iota(jnp.int32, (SHARE, 512), 0)
     doc = lax.broadcasted_iota(jnp.int32, (8, 512), 1).astype(F32)
     doc_slot = split_slots(doc)[1]
@@ -266,8 +267,7 @@
         enters.astype(BF16), begun.astype(F32).astype(BF16), NT, preferred_element_type=F32
     )
 
-    for copy in proj_copies:
-        copy.wait_recv()
+    drain(proj_recv, p_recv)
     proj = proj_own[...]
     for t in range(2):
         proj = proj + proj_recv[t].astype(F32)
@@ -326,7 +326,7 @@
     first = jnp.broadcast_to(starts, (8, 512)) // SHARE
     last = jnp.where(lane8 == 511, DEVICES - 1, pltpu.roll(first, 511, 1))
     facts = jnp.where(row8 == 0, first.astype(F32), jnp.where(row8 == 1, last.astype(F32), doc_slot))
-    rank = owner_ref[...] * 16 + lax.broadcasted_iota(jnp.int32, (1, 512), 1) // 32
+    rank = docs_ref[1] * 16 + lax.broadcasted_iota(jnp.int32, (1, 512), 1) // 32
     perm = (rank == lax.broadcasted_iota(jnp.int32, (512, 512), 0)).astype(F32).astype(BF16)
     ranked = lax.dot_general(perm, facts.astype(BF16), NT, preferred_element_type=F32)
     block, slot = split_slots(lax.broadcasted_iota(jnp.int32, (8, 32 * SLOTS), 1).astype(F32))
@@ -344,7 +344,7 @@
     for n in (2, 3, 1, 0):
         g = (z + n) % 4
         got = wnd_recv.at[g, pl.ds(0, (32 if n else 31) * PAIRS)]
-        pltpu.make_async_copy(got, got, d_recv.at[g]).wait()
+        drain(got, d_recv.at[g])
         summed = summed + jnp.dot(
             place[g], wnd_recv[g].reshape(32 * SLOTS, 128), preferred_element_type=F32
         )
@@ -357,12 +357,12 @@
         ty, tz = (y + n) % 4, (z + n) % 4
         u_copies.append(
             remote(
-                units.at[tz], vb.at[:, :, at_z], u_send.at[1, n - 1], u_recv.at[1, n - 1], tz * 8 + y * 2 + c, pb
+                units.at[tz], vb.at[:, :, at_z], u_send, u_recv.at[1], tz * 8 + y * 2 + c, pb
             )
         )
         u_copies.append(
             remote(
-                units.at[:, ty], va.at[:, :, at_y], u_send.at[0, n - 1], u_recv.at[0, n - 1], z * 8 + ty * 2 + c, pb
+                units.at[:, ty], va.at[:, :, at_y], u_send, u_recv.at[0], z * 8 + ty * 2 + c, pb
             )
         )
     for copy in u_copies:
@@ -371,14 +371,12 @@
     vb[:, :, at_z] = units[z]
     fa_me, fb_me = z * 2 + c, y * 2 + c
 
-    for copy in q_second + q_passed:
-        copy.wait_recv()
+    drain(q_all.at[0], qs_recv.at[1])
     for n in range(4):
-        qa_t[pl.ds(n * 128, 128), :] = qa[n].T
-        qb_t[pl.ds(n * 128, 128), :] = qb[n].T
-
-    for copy in u_copies[0::2]:
-        copy.wait_recv()
+        qa_t[pl.ds(n * 128, 128), :] = q_all[0, n].T
+        qb_t[pl.ds(n * 128, 128), :] = q_all[1, n].T
+
+    drain(vb.at[:, :, pl.ds(0, 384)], u_recv.at[1])
     fb[...] = jnp.dot(vb[...].reshape(128, 512), qb_t[...], preferred_element_type=F32).astype(BF16)
 
     @pl.loop(1, 8)
@@ -387,14 +385,13 @@
         remote(
             fb.at[pl.ds(pl.multiple_of(to * 16, 16), 16)],
             fb_recv.at[fb_me],
-            f_send.at[1],
+            f_send,
             f_recv.at[1],
             z * 8 + to,
             pb,
         ).start()
 
-    for copy in u_copies[1::2]:
-        copy.wait_recv()
+    drain(va.at[:, :, pl.ds(0, 384)], u_recv.at[0])
     docs = va[...].reshape(128, 512)
     fa[:, :1024] = jnp.dot(docs, qa_t[...], preferred_element_type=F32).astype(BF16)
     wide = docs.astype(F32)
@@ -410,7 +407,7 @@
         remote(
             fa.at[pl.ds(pl.multiple_of(to * 16, 16), 16)],
             fa_recv.at[fa_me],
-            f_send.at[0],
+            f_send,
             f_recv.at[0],
             (to // 2) * 8 + y * 2 + to % 2,
             pb,
@@ -418,11 +415,11 @@
 
     fa_recv[fa_me] = fa[pl.ds(pl.multiple_of(fa_me * 16, 16), 16), :]
     fb_recv[fb_me] = fb[pl.ds(pl.multiple_of(fb_me * 16, 16), 16), :]
-    pltpu.make_async_copy(fb_recv.at[pl.ds(0, 7)], fb_recv.at[pl.ds(0, 7)], f_recv.at[1]).wait()
+    drain(fb_recv.at[pl.ds(0, 7)], f_recv.at[1])
     total_b = fb_recv[0].astype(F32)
     for n in range(1, 8):
         total_b = total_b + fb_recv[n].astype(F32)
-    pltpu.make_async_copy(fa_recv.at[pl.ds(0, 7)], fa_recv.at[pl.ds(0, 7)], f_recv.at[0]).wait()
+    drain(fa_recv.at[pl.ds(0, 7)], f_recv.at[0])
     total_a = fa_recv[0].astype(F32)
     for n in range(1, 8):
         total_a = total_a + fa_recv[n].astype(F32)
@@ -431,13 +428,14 @@
     out_ref[:, :1024] = total_a[:, :1024] * norm
     out_ref[:, 1024:] = total_b * norm
 
-    for copy in relay_copies + proj_copies + q_copies + u_copies:
-        copy.wait_send()
+    drain(proj_send, p_send)
+    drain(q_all.at[:, pl.ds(0, 3)], qs_send)
+    for n in range(2):
+        drain(va.at[:, :, pl.ds(0, 384)], u_send)
     for g in range(4):
-        some = wnd.at[pl.ds(0, (32 if g else 31) * PAIRS)]
-        pltpu.make_async_copy(some, some, d_send).wait()
-    pltpu.make_async_copy(fa.at[pl.ds(0, 112)], fa.at[pl.ds(0, 112)], f_send.at[0]).wait()
-    pltpu.make_async_copy(fb.at[pl.ds(0, 112)], fb.at[pl.ds(0, 112)], f_send.at[1]).wait()
+        drain(wnd.at[pl.ds(0, (32 if g else 31) * PAIRS)], d_send)
+    drain(fa.at[pl.ds(0, 112)], f_send)
+    drain(fb.at[pl.ds(0, 112)], f_send)
 
 
 def per_device(activations, out_grads, proj_in, proj_out, doc_starts, doc_owner, queries):
@@ -454,12 +452,9 @@
         in_specs=[pl.BlockSpec(memory_space=pltpu.HBM)] * 7,
         out_specs=pl.BlockSpec(memory_space=pltpu.VMEM),
         scratch_shapes=[
-            vmem((4, SHARE, depth_in), BF16),
-            vmem((4, SHARE, depth_out), BF16),
-            vmem((64, depth_in), BF16),
-            vmem((64, depth_out), BF16),
-            vmem((1, 512), jnp.int32),
-            vmem((1, 512), jnp.int32),
+            vmem((4, SHARE, depth_in + depth_out), BF16),
+            vmem((128, depth_in + depth_out), BF16),
+            vmem((2, 1, 512), jnp.int32),
             vmem((3, SHARE, 128), BF16),
             vmem((SHARE, 128), F32),
             vmem((2, SHARE, 128), BF16),
@@ -473,26 +468,27 @@
             vmem((4, 4, 32, 128), BF16),
             vmem((4, 32, 512), BF16),
             vmem((4, 32, 512), BF16),
-            vmem((4, 1024, 128), BF16),
-            vmem((4, 1024, 128), BF16),
+            vmem((2, 4, 1024, 128), BF16),
             vmem((512, 1024), BF16),
             vmem((512, 1024), BF16),
             vmem((128, 1152), BF16),
             vmem((128, 1024), BF16),
             vmem((8, 16, 1152), BF16),
             vmem((8, 16, 1024), BF16),
-            dma((2, 7)),
+            dma((7,)),
+            dma,
+            dma,
+            dma,
+            dma,
+            dma((2,)),
+            dma,
+            dma((2,)),
+            dma,
+            dma,
             dma((4,)),
+            dma,
             dma((2,)),
-            dma((2, 6)),
-            dma((2, 6)),
-            dma((6,)),
-            dma((6,)),
-            dma,
-            dma((4,)),
-            dma((2, 3)),
-            dma((2, 3)),
-            dma((2,)),
+            dma,
             dma((2,)),
             pltpu.SemaphoreType.REGULAR((3,)),
         ],

time: 36.9 us -> 36.3 us (0.984)
  Pallas kernels: 36.2 us -> 35.5 us
    pallas_call x1, Pallas kernels: 36.2 us -> 35.5 us  [per_device(): pl.pallas_call(kernel, out_shape=jax.ShapeDtypeStruct((16, 2048), F32), i...]
where the time goes in v6:
time: 36.3 us; the launch traced here: 36.2 us
  Pallas kernels  35.5 us (98%)
  local copies, waits for them, and re-layouts  0.66 us (2%)
    pallas_call x1, Pallas kernels, per_device(): pl.pallas_call(kernel, out_shape=jax.ShapeDtypeStruct((16, 2048), F32), i...  35.5 us

profile of v6, /device:TPU:1, one launch (start us, length us, event | category | flops | bytes accessed | tf_op | source)
XLA Modules:
  0.0 36.2 jit_solution(3196613871667376920)
XLA Ops:
  0.0 35.5 %shard_map.73 = f32[16,2048]{1,0:T(8,128)S(1)} custom-call(bf16[2048,3584]{1,0:T(8,128)(2,1)} %act_hbm.1, bf16[2048,1024]{1,0:T(8,128)(2,1)} %grad_hbm.1, bf16[64,3584]{1,0:T(8,128)(2,1)} %bitcast.4, bf16[64,1024]{1,0:T(8,128)(2,1)} %bitcast.5, s32[1,512]{1,0:T(1,128)} %bitcast.6, s32[1,512]{1,0:T(1,128)} %bitcast.7, bf16[2048,128]{1,0:T(8,128)(2,1)} %q_hbm.1), custom_call_target="tpu_custom_call" | custom-call | tf_op jit(solution)/shard_map/pallas_call | solution.py:449
  35.5 0.7 %copy.9 = f32[16,2048]{1,0:T(8,128)} copy(f32[16,2048]{1,0:T(8,128)S(1)} %shard_map.73) | data formatting | bytes 262144

commit v7 on v6

--- a/solution.py
+++ b/solution.py
@@ -102,23 +102,23 @@
     depth_out = grad_hbm.shape[1]
     of_act, of_grad = pl.ds(0, depth_in), pl.ds(depth_in, depth_out)
 
-    def loads_of(rows, t, at, sem):
+    def loads_of(hop, half, t, at, sem):
+        rows = pl.ds(pl.multiple_of(lax.rem(pb + hop, 4) * SHARE + half * HALF, HALF), HALF)
         return [
             pltpu.make_async_copy(grad_hbm.at[rows], tokens.at[t, at, of_grad], load_sem.at[sem]),
             pltpu.make_async_copy(act_hbm.at[rows], tokens.at[t, at, of_act], load_sem.at[sem]),
         ]
 
-    def half_of(s):
-        t = jnp.where(s < 2, 0, 1 + lax.rem(s, 2))
-        h = jnp.where((s == 0) | (s == 3) | (s == 4), 0, 1)
-        return t, pl.ds(pl.multiple_of(h * HALF, HALF), HALF), h
-
-    def half_loads(s):
-        t, at, h = half_of(s)
-        start = lax.rem(pb + hop_of(t), 4) * SHARE + h * HALF
-        return loads_of(pl.ds(pl.multiple_of(start, HALF), HALF), t, at, s)
-
-    own_loads = loads_of(pl.ds(pl.multiple_of(pb * SHARE, SHARE), SHARE), 3, pl.ds(0, SHARE), 6)
+    def far_half(s):
+        return pl.ds(pl.multiple_of(s * HALF, HALF), HALF)
+
+    first_half, second_half = pl.ds(0, HALF), pl.ds(HALF, HALF)
+
+    def full_loads(t):
+        return loads_of(jnp.where(t == 3, 0, 1), jnp.where(t == 1, 1, 0), t, first_half, t + 1) + loads_of(
+            jnp.where(t == 3, 0, 3), jnp.where(t == 1, 0, 1), t, second_half, t + 1
+        )
+
     small = [
         pltpu.make_async_copy(wout_hbm, weights.at[pl.ds(64, 64), of_grad], w_sem),
         pltpu.make_async_copy(win_hbm, weights.at[pl.ds(0, 64), of_act], w_sem),
@@ -131,16 +131,14 @@
     ]
     small[0].start()
     small[1].start()
-    for copy in half_loads(0) + q_loads:
+    for copy in loads_of(2, 0, 0, first_half, 0) + q_loads + loads_of(2, 1, 0, second_half, 1):
         copy.start()
 
-    @pl.loop(1, 6)
-    def _(s):
-        for copy in half_loads(s):
+    @pl.loop(1, 4)
+    def _(t):
+        for copy in full_loads(t):
             copy.start()
 
-    for copy in own_loads:
-        copy.start()
     small[2].start()
     small[3].start()
 
@@ -184,71 +182,78 @@
 
     def relay_copy(s):
         return remote(
-            proj_send.at[0, half_of(s)[1]],
-            proj_relay.at[s],
+            proj_send.at[0, far_half(s)],
+            proj_relay.at[far_half(s)],
             p_send,
-            relay_recv.at[s],
+            relay_recv,
             tok,
             lax.rem(pb + 1 + 2 * s, 4),
         )
 
-    def proj_copy(s):
-        t, at, _ = half_of(s)
-        return remote(
-            proj_send.at[t, at], proj_recv.at[t - 1, at], p_send, p_recv, tok, lax.rem(pb + hop_of(t), 4)
-        )
-
-    @pl.loop(0, 6)
+    def proj_copies(t):
+        return [
+            remote(
+                proj_send.at[t, at],
+                proj_recv.at[n, pl.ds(pl.multiple_of(half * HALF, HALF), HALF)],
+                p_send,
+                p_recv,
+                tok,
+                lax.rem(pb + 1 + 2 * n, 4),
+            )
+            for n, at, half in ((0, first_half, 2 - t), (1, second_half, t - 1))
+        ]
+
+    @pl.loop(0, 2)
     def _(s):
-        t, at, _ = half_of(s)
-        drain(tokens.at[t, at], load_sem.at[s])
-        both = project(t, at)
-
-        @pl.when(s < 4)
-        def _():
-            proj_send[t, at, :] = both.astype(BF16)
+        drain(tokens.at[0, far_half(s)], load_sem.at[s])
+        proj_send[0, far_half(s), :] = project(0, far_half(s)).astype(BF16)
 
         @pl.when(s == 0)
         def _():
             pl.semaphore_wait(barrier, 10)
             signal(round_sem.at[0], on_y)
 
-        @pl.when(s < 2)
-        def _():
-            relay_copy(s).start()
-
-        @pl.when(s == 2)
+        relay_copy(s).start()
+
+        @pl.when(s == 0)
+        def _():
+            drain(q_all.at[0, pl.ds(0, 2)], q_sem)
+            for copy in q_first + q_second:
+                copy.start()
+
+    @pl.loop(1, 4)
+    def _(t):
+        drain(tokens.at[t], load_sem.at[t + 1])
+        both = project(t, pl.ds(0, SHARE))
+
+        @pl.when(t == 1)
+        def _():
+            proj_send[1] = both.astype(BF16)
+
+        @pl.when(t == 2)
+        def _():
+            drain(proj_relay, relay_recv)
+            proj_send[2] = (both + proj_relay[...].astype(F32)).astype(BF16)
+
+        @pl.when(t < 3)
+        def _():
+            for copy in proj_copies(t):
+                copy.start()
+
+        @pl.when(t == 1)
         def _():
             pl.semaphore_wait(round_sem.at[0], 3)
             signal(round_sem.at[1], on_z)
 
-        @pl.when(s == 4)
+        @pl.when(t == 2)
         def _():
             pl.semaphore_wait(round_sem.at[1], 3)
             signal(round_sem.at[2], on_core)
 
-        @pl.when(s >= 4)
-        def _():
-            drain(proj_relay.at[s - 4], relay_recv.at[s - 4])
-            proj_send[t, at, :] = (both + proj_relay[s - 4].astype(F32)).astype(BF16)
-
-        @pl.when(s >= 2)
-        def _():
-            proj_copy(s).start()
-
-        @pl.when(s == 0)
-        def _():
-            drain(q_all.at[0, pl.ds(0, 2)], q_sem)
-            for copy in q_first:
-                copy.start()
-
-        @pl.when(s == 0)
-        def _():
-            for copy in q_second:
-                copy.start()
-
-    drain(tokens.at[3], load_sem.at[6])
-    proj_own[...] = project(3, pl.ds(0, SHARE))
+        @pl.when(t == 3)
+        def _():
+            proj_own[...] = both
+
     pl.semaphore_wait(round_sem.at[2], 1)
     drain(q_all.at[0, pl.ds(0, 2)], qs_recv.at[0])
     for copy in q_passed:
@@ -458,7 +463,7 @@
             vmem((3, SHARE, 128), BF16),
             vmem((SHARE, 128), F32),
             vmem((2, SHARE, 128), BF16),
-            vmem((2, HALF, 128), BF16),
+            vmem((SHARE, 128), BF16),
             vmem((GROUP, SHARE), F32),
             vmem((4, 512, 32 * SLOTS), BF16),
             vmem((GROUP, 2 * SHARE), BF16),
@@ -475,14 +480,14 @@
             vmem((128, 1024), BF16),
             vmem((8, 16, 1152), BF16),
             vmem((8, 16, 1024), BF16),
-            dma((7,)),
+            dma((5,)),
             dma,
             dma,
             dma,
             dma,
             dma((2,)),
             dma,
-            dma((2,)),
+            dma,
             dma,
             dma,
             dma((4,)),

time: 36.3 us -> 35.8 us (0.986)
  Pallas kernels: 35.5 us -> 35 us
    pallas_call x1, Pallas kernels: 35.5 us -> 35 us  [per_device(): pl.pallas_call(kernel, out_shape=jax.ShapeDtypeStruct((16, 2048), F32), i...]
where the time goes in v7:
time: 35.8 us; the launch traced here: 35.7 us
  Pallas kernels  35 us (98%)
  local copies, waits for them, and re-layouts  0.66 us (2%)
    pallas_call x1, Pallas kernels, per_device(): pl.pallas_call(kernel, out_shape=jax.ShapeDtypeStruct((16, 2048), F32), i...  35 us

profile of v7, /device:TPU:1, one launch (start us, length us, event | category | flops | bytes accessed | tf_op | source)
XLA Modules:
  0.0 35.7 jit_solution(10562389003754685752)
XLA Ops:
  0.0 35.0 %shard_map.73 = f32[16,2048]{1,0:T(8,128)S(1)} custom-call(bf16[2048,3584]{1,0:T(8,128)(2,1)} %act_hbm.1, bf16[2048,1024]{1,0:T(8,128)(2,1)} %grad_hbm.1, bf16[64,3584]{1,0:T(8,128)(2,1)} %bitcast.4, bf16[64,1024]{1,0:T(8,128)(2,1)} %bitcast.5, s32[1,512]{1,0:T(1,128)} %bitcast.6, s32[1,512]{1,0:T(1,128)} %bitcast.7, bf16[2048,128]{1,0:T(8,128)(2,1)} %q_hbm.1), custom_call_target="tpu_custom_call" | custom-call | tf_op jit(solution)/shard_map/pallas_call | solution.py:454
  35.0 0.7 %copy.9 = f32[16,2048]{1,0:T(8,128)} copy(f32[16,2048]{1,0:T(8,128)S(1)} %shard_map.73) | data formatting | bytes 262144

commit v8 on v7

--- a/solution.py
+++ b/solution.py
@@ -187,7 +187,7 @@
             p_send,
             relay_recv,
             tok,
-            lax.rem(pb + 1 + 2 * s, 4),
+            lax.rem(pb + 2, 4),
         )
 
     def proj_copies(t):
@@ -226,17 +226,9 @@
         drain(tokens.at[t], load_sem.at[t + 1])
         both = project(t, pl.ds(0, SHARE))
 
-        @pl.when(t == 1)
-        def _():
-            proj_send[1] = both.astype(BF16)
-
-        @pl.when(t == 2)
-        def _():
-            drain(proj_relay, relay_recv)
-            proj_send[2] = (both + proj_relay[...].astype(F32)).astype(BF16)
-
         @pl.when(t < 3)
         def _():
+            proj_send[t] = both.astype(BF16)
             for copy in proj_copies(t):
                 copy.start()
 
@@ -272,8 +264,9 @@
         enters.astype(BF16), begun.astype(F32).astype(BF16), NT, preferred_element_type=F32
     )
 
+    drain(proj_relay, relay_recv)
+    proj = proj_own[...] + proj_relay[...].astype(F32)
     drain(proj_recv, p_recv)
-    proj = proj_own[...]
     for t in range(2):
         proj = proj + proj_recv[t].astype(F32)
     proj = proj.astype(BF16)
@@ -357,17 +350,20 @@
 
     at_y = pl.ds(pl.multiple_of(y * 128, 128), 128)
     at_z = pl.ds(pl.multiple_of(z * 128, 128), 128)
+    def other(n, mine):
+        return n + jnp.where(n >= mine, 1, 0)
+
     u_copies = []
-    for n in range(1, 4):
-        ty, tz = (y + n) % 4, (z + n) % 4
+    for n in range(3):
+        ty, tz = other(n, y), other(n, z)
         u_copies.append(
             remote(
-                units.at[tz], vb.at[:, :, at_z], u_send, u_recv.at[1], tz * 8 + y * 2 + c, pb
+                units.at[:, ty], va.at[:, :, at_y], u_send, u_recv.at[0], z * 8 + ty * 2 + c, pb
             )
         )
         u_copies.append(
             remote(
-                units.at[:, ty], va.at[:, :, at_y], u_send, u_recv.at[0], z * 8 + ty * 2 + c, pb
+                units.at[tz], vb.at[:, :, at_z], u_send, u_recv.at[1], tz * 8 + y * 2 + c, pb
             )
         )
     for copy in u_copies:
@@ -380,21 +376,6 @@
     for n in range(4):
         qa_t[pl.ds(n * 128, 128), :] = q_all[0, n].T
         qb_t[pl.ds(n * 128, 128), :] = q_all[1, n].T
-
-    drain(vb.at[:, :, pl.ds(0, 384)], u_recv.at[1])
-    fb[...] = jnp.dot(vb[...].reshape(128, 512), qb_t[...], preferred_element_type=F32).astype(BF16)
-
-    @pl.loop(1, 8)
-    def _(n):
-        to = (fb_me + n) % 8
-        remote(
-            fb.at[pl.ds(pl.multiple_of(to * 16, 16), 16)],
-            fb_recv.at[fb_me],
-            f_send,
-            f_recv.at[1],
-            z * 8 + to,
-            pb,
-        ).start()
 
     drain(va.at[:, :, pl.ds(0, 384)], u_recv.at[0])
     docs = va[...].reshape(128, 512)
@@ -406,24 +387,35 @@
         lax.broadcasted_iota(jnp.int32, (128, 128), 1) < 64, high, square - high
     ).astype(BF16)
 
-    @pl.loop(1, 8)
+    @pl.loop(0, 7)
     def _(n):
-        to = (fa_me + n) % 8
+        to = other(n, fa_me)
         remote(
             fa.at[pl.ds(pl.multiple_of(to * 16, 16), 16)],
             fa_recv.at[fa_me],
             f_send,
             f_recv.at[0],
-            (to // 2) * 8 + y * 2 + to % 2,
+            lax.div(to, 2) * 8 + y * 2 + lax.rem(to, 2),
             pb,
         ).start()
 
+    drain(vb.at[:, :, pl.ds(0, 384)], u_recv.at[1])
+    fb[...] = jnp.dot(vb[...].reshape(128, 512), qb_t[...], preferred_element_type=F32).astype(BF16)
+
+    @pl.loop(0, 7)
+    def _(n):
+        to = other(n, fb_me)
+        remote(
+            fb.at[pl.ds(pl.multiple_of(to * 16, 16), 16)],
+            fb_recv.at[fb_me],
+            f_send,
+            f_recv.at[1],
+            z * 8 + to,
+            pb,
+        ).start()
+
     fa_recv[fa_me] = fa[pl.ds(pl.multiple_of(fa_me * 16, 16), 16), :]
     fb_recv[fb_me] = fb[pl.ds(pl.multiple_of(fb_me * 16, 16), 16), :]
-    drain(fb_recv.at[pl.ds(0, 7)], f_recv.at[1])
-    total_b = fb_recv[0].astype(F32)
-    for n in range(1, 8):
-        total_b = total_b + fb_recv[n].astype(F32)
     drain(fa_recv.at[pl.ds(0, 7)], f_recv.at[0])
     total_a = fa_recv[0].astype(F32)
     for n in range(1, 8):
@@ -431,6 +423,10 @@
     tail = total_a[:, 1024:]
     norm = lax.rsqrt(tail + pltpu.roll(tail, 64, 1) + EPS)[:, 0:1]
     out_ref[:, :1024] = total_a[:, :1024] * norm
+    drain(fb_recv.at[pl.ds(0, 7)], f_recv.at[1])
+    total_b = fb_recv[0].astype(F32)
+    for n in range(1, 8):
+        total_b = total_b + fb_recv[n].astype(F32)
     out_ref[:, 1024:] = total_b * norm
 
     drain(proj_send, p_send)

time: 35.8 us -> 35 us (0.978)
  Pallas kernels: 35 us -> 34.2 us
    pallas_call x1, Pallas kernels: 35 us -> 34.2 us  [per_device(): pl.pallas_call(kernel, out_shape=jax.ShapeDtypeStruct((16, 2048), F32), i...]
where the time goes in v8:
time: 35 us; the launch traced here: 34.9 us
  Pallas kernels  34.2 us (98%)
  local copies, waits for them, and re-layouts  0.66 us (2%)
    pallas_call x1, Pallas kernels, per_device(): pl.pallas_call(kernel, out_shape=jax.ShapeDtypeStruct((16, 2048), F32), i...  34.2 us

profile of v8, /device:TPU:1, one launch (start us, length us, event | category | flops | bytes accessed | tf_op | source)
XLA Modules:
  0.0 34.9 jit_solution(6715658303302548925)
XLA Ops:
  0.0 34.2 %shard_map.73 = f32[16,2048]{1,0:T(8,128)S(1)} custom-call(bf16[2048,3584]{1,0:T(8,128)(2,1)} %act_hbm.1, bf16[2048,1024]{1,0:T(8,128)(2,1)} %grad_hbm.1, bf16[64,3584]{1,0:T(8,128)(2,1)} %bitcast.4, bf16[64,1024]{1,0:T(8,128)(2,1)} %bitcast.5, s32[1,512]{1,0:T(1,128)} %bitcast.6, s32[1,512]{1,0:T(1,128)} %bitcast.7, bf16[2048,128]{1,0:T(8,128)(2,1)} %q_hbm.1), custom_call_target="tpu_custom_call" | custom-call | tf_op jit(solution)/shard_map/pallas_call | solution.py:450
  34.2 0.7 %copy.9 = f32[16,2048]{1,0:T(8,128)} copy(f32[16,2048]{1,0:T(8,128)S(1)} %shard_map.73) | data formatting | bytes 262144

commit v9 on v8

--- a/solution.py
+++ b/solution.py
@@ -389,7 +389,8 @@
 
     @pl.loop(0, 7)
     def _(n):
-        to = other(n, fa_me)
+        k = other(n, z * 2 + 1 - c)
+        to = k + 1 - 2 * lax.rem(k, 2)
         remote(
             fa.at[pl.ds(pl.multiple_of(to * 16, 16), 16)],
             fa_recv.at[fa_me],
@@ -404,7 +405,8 @@
 
     @pl.loop(0, 7)
     def _(n):
-        to = other(n, fb_me)
+        k = other(n, y * 2 + 1 - c)
+        to = k + 1 - 2 * lax.rem(k, 2)
         remote(
             fb.at[pl.ds(pl.multiple_of(to * 16, 16), 16)],
             fb_recv.at[fb_me],

time: 35 us -> 34.5 us (0.986)
  Pallas kernels: 34.2 us -> 33.8 us
    pallas_call x1, Pallas kernels: 34.2 us -> 33.8 us  [per_device(): pl.pallas_call(kernel, out_shape=jax.ShapeDtypeStruct((16, 2048), F32), i...]
where the time goes in v9:
time: 34.5 us; the launch traced here: 34.4 us
  Pallas kernels  33.8 us (98%)
  local copies, waits for them, and re-layouts  0.66 us (2%)
    pallas_call x1, Pallas kernels, per_device(): pl.pallas_call(kernel, out_shape=jax.ShapeDtypeStruct((16, 2048), F32), i...  33.8 us

profile of v9, /device:TPU:1, one launch (start us, length us, event | category | flops | bytes accessed | tf_op | source)
XLA Modules:
  0.0 34.4 jit_solution(5106216089464633669)
XLA Ops:
  0.0 33.8 %shard_map.73 = f32[16,2048]{1,0:T(8,128)S(1)} custom-call(bf16[2048,3584]{1,0:T(8,128)(2,1)} %act_hbm.1, bf16[2048,1024]{1,0:T(8,128)(2,1)} %grad_hbm.1, bf16[64,3584]{1,0:T(8,128)(2,1)} %bitcast.4, bf16[64,1024]{1,0:T(8,128)(2,1)} %bitcast.5, s32[1,512]{1,0:T(1,128)} %bitcast.6, s32[1,512]{1,0:T(1,128)} %bitcast.7, bf16[2048,128]{1,0:T(8,128)(2,1)} %q_hbm.1), custom_call_target="tpu_custom_call" | custom-call | tf_op jit(solution)/shard_map/pallas_call | solution.py:452
  33.8 0.7 %copy.9 = f32[16,2048]{1,0:T(8,128)} copy(f32[16,2048]{1,0:T(8,128)S(1)} %shard_map.73) | data formatting | bytes 262144

commit v10 on v9

--- a/solution.py
+++ b/solution.py
@@ -279,7 +279,6 @@
         [jnp.where(low, wide, 0.0), jnp.where(low, 0.0, pltpu.roll(wide, 64, 1))], axis=0
     ).astype(BF16)
     mine = pl.ds(lax.rem(me, 32) * PAIRS, PAIRS)
-    far_planes = [planes[2], planes[1], planes[3], planes[0]]
 
     def send_block(to, plane):
         remote(
@@ -305,18 +304,16 @@
         @pl.loop(0, 3)
         def _(n):
             row = g * 8 + lax.rem(y + hop_of(n), 4) * 2
-            for plane in far_planes:
+            for plane in range(4):
                 send_block(row + c, plane)
                 send_block(row + 1 - c, plane)
 
-        for plane in far_planes[:3]:
-            send_block(g * 8 + y * 2 + c, plane)
+        for plane in range(4):
             send_block(g * 8 + y * 2 + 1 - c, plane)
-        send_block(g * 8 + y * 2 + 1 - c, pb)
-
-        @pl.when(k < 3)
-        def _():
-            send_block(g * 8 + y * 2 + c, pb)
+
+            @pl.when((k < 3) | (pb != plane))
+            def _():
+                send_block(g * 8 + y * 2 + c, plane)
 
     wnd_recv[z, mine] = wnd[pl.ds(tok * PAIRS, PAIRS)]
     lane8 = lax.broadcasted_iota(jnp.int32, (8, 512), 1)

time: 34.5 us -> 34.3 us (level)
  no operation moved by 1% of the time
where the time goes in v10:
time: 34.3 us; the launch traced here: 34.2 us
  Pallas kernels  33.5 us (98%)
  local copies, waits for them, and re-layouts  0.66 us (2%)
    pallas_call x1, Pallas kernels, per_device(): pl.pallas_call(kernel, out_shape=jax.ShapeDtypeStruct((16, 2048), F32), i...  33.5 us

profile of v10, /device:TPU:1, one launch (start us, length us, event | category | flops | bytes accessed | tf_op | source)
XLA Modules:
  0.0 34.2 jit_solution(17490209108241121101)
XLA Ops:
  0.0 33.5 %shard_map.73 = f32[16,2048]{1,0:T(8,128)S(1)} custom-call(bf16[2048,3584]{1,0:T(8,128)(2,1)} %act_hbm.1, bf16[2048,1024]{1,0:T(8,128)(2,1)} %grad_hbm.1, bf16[64,3584]{1,0:T(8,128)(2,1)} %bitcast.4, bf16[64,1024]{1,0:T(8,128)(2,1)} %bitcast.5, s32[1,512]{1,0:T(1,128)} %bitcast.6, s32[1,512]{1,0:T(1,128)} %bitcast.7, bf16[2048,128]{1,0:T(8,128)(2,1)} %q_hbm.1), custom_call_target="tpu_custom_call" | custom-call | tf_op jit(solution)/shard_map/pallas_call | solution.py:449
  33.6 0.7 %copy.9 = f32[16,2048]{1,0:T(8,128)} copy(f32[16,2048]{1,0:T(8,128)S(1)} %shard_map.73) | data formatting | bytes 262144
